TPU v7x, 32 devices: a whole 2x2x4 slice. The times are simulated.
32 devices in a mesh: dp: 8 (over y, x, core), blk: 4 (over z).
Axes of the slice: x: 2, y: 2, z: 4, core: 2. Of those that a mesh axis runs over, the one named last changes fastest.
Arguments:
- clips: bfloat16 [64, 8, 8, 8, 528], P('dp', 'blk'), may hold values from -19 to 19
- cotangent: bfloat16 [64, 4, 4, 4, 832], P('dp', 'blk'), may hold values from -19 to 19
- entry_4f: bfloat16 [2, 236544], P(None, 'blk'), may hold values from -0.25 to 0.25
- wide_4f: bfloat16 [2, 1382400], P(None, 'blk'), may hold values from -0.09375 to 0.09375
- narrow_4f: bfloat16 [2, 110592], P(None, 'blk'), may hold values from -0.21875 to 0.21875
- poolproj_4f: bfloat16 [2, 67584], P(None, 'blk'), may hold values from -0.25 to 0.25
- gain_4f: bfloat16 [2, 1024], P(None, 'blk'), may hold values from 0.099609375 to 1.8984375
- shift_4f: bfloat16 [2, 1024], P(None, 'blk'), may hold values from -2.5 to 2.5
- entry_5b: bfloat16 [2, 372736], P(None, 'blk'), may hold values from -0.21875 to 0.21875
- wide_5b: bfloat16 [2, 1382400], P(None, 'blk'), may hold values from -0.09375 to 0.09375
- narrow_5b: bfloat16 [2, 110592], P(None, 'blk'), may hold values from -0.21875 to 0.21875
- poolproj_5b: bfloat16 [2, 106496], P(None, 'blk'), may hold values from -0.21875 to 0.21875
- gain_5b: bfloat16 [2, 1024], P(None, 'blk'), may hold values from 0.099609375 to 1.8984375
- shift_5b: bfloat16 [2, 1024], P(None, 'blk'), may hold values from -2.5 to 2.5
Outputs:
- features: float32 [64, 4, 4, 4, 832], P('dp', 'blk')
- clips_grad: float32 [64, 8, 8, 8, 528], P('dp', 'blk')
- entry_4f_grad: float32 [2, 236544], P(None, 'blk')
- wide_4f_grad: float32 [2, 1382400], P(None, 'blk')
- narrow_4f_grad: float32 [2, 110592], P(None, 'blk')
- poolproj_4f_grad: float32 [2, 67584], P(None, 'blk')
- gain_4f_grad: float32 [2, 1024], P(None, 'blk')
- shift_4f_grad: float32 [2, 1024], P(None, 'blk')
- entry_5b_grad: float32 [2, 372736], P(None, 'blk')
- wide_5b_grad: float32 [2, 1382400], P(None, 'blk')
- narrow_5b_grad: float32 [2, 110592], P(None, 'blk')
- poolproj_5b_grad: float32 [2, 106496], P(None, 'blk')
- gain_5b_grad: float32 [2, 1024], P(None, 'blk')
- shift_5b_grad: float32 [2, 1024], P(None, 'blk')
All inputs are finite; a program needn't handle non-finite values.
Results may differ from a plain program's by a relative error of at most 0.022.
Values may be sent and summed in bfloat16 or wider, within the bound.
No kernel may reach another device: no remote copies, remote signals or barrier semaphores. Data moves between devices by JAX's collectives and lax.ppermute only.
A program may use at most 256 MiB of HBM per device.

v0:
```python
import functools

import jax
import jax.numpy as jnp
from jax import lax
from jax.experimental import pallas as pl
from jax.experimental.pallas import tpu as pltpu
from jax.sharding import PartitionSpec as P

B0 = 256
B1R = 160
B1 = 320
B2R = 32
B2 = 128
BP = 128
INNER = B1R + B2R
REDUCED = B0 + INNER
OUTER = B1 + B2
LAYER = B0 + OUTER + BP
EPS = 1e-05
BF = jnp.bfloat16
F32 = jnp.float32
TAPS = 27
NARROW_AT = 896
POOL_LANE = 64

NT = (((1,), (1,)), ((), ()))
NN = (((1,), (0,)), ((), ()))
VMEM = pl.BlockSpec(memory_space=pltpu.VMEM)
SMEM = pl.BlockSpec(memory_space=pltpu.SMEM)


def mm(a, b, dims=NN):
    return lax.dot_general(a, b, dims, preferred_element_type=F32)


def shape_of(shape, kind=F32):
    return jax.ShapeDtypeStruct(shape, kind)


def call(body, outs, *args, micros=2, scratch=(), mib=6, lazy=(), away=()):
    def whole(*refs):
        bufs, sems = refs[len(refs) - len(lazy) - 1 : -1], refs[-1]
        copies = [
            pltpu.make_async_copy(refs[i], bufs[n], sems.at[n]) for n, i in enumerate(lazy)
        ]
        for copy in copies:
            copy.start()
        for copy in copies:
            copy.wait()
        ins = list(refs[: len(args)])
        for n, i in enumerate(lazy):
            ins[i] = bufs[n]
        body(*ins, *refs[len(args) : len(refs) - len(lazy) - 1])

    lazy = [i % len(args) for i in lazy]
    specs = [SMEM if a.dtype == jnp.int32 else VMEM for a in args]
    scratch, size = list(scratch), 0
    for i in lazy:
        specs[i] = pl.BlockSpec(memory_space=pl.ANY)
        scratch.append(pltpu.VMEM(args[i].shape, args[i].dtype))
        size += args[i].size * args[i].dtype.itemsize
    if lazy:
        scratch.append(pltpu.SemaphoreType.DMA((len(lazy),)))
    spots = [VMEM] * (len(outs) if isinstance(outs, tuple) else 1)
    for i in away:
        spots[i] = pl.BlockSpec(memory_space=pltpu.HBM)
    return pl.pallas_call(
        whole if lazy else body,
        out_shape=outs,
        in_specs=specs,
        out_specs=spots if isinstance(outs, tuple) else spots[0],
        scratch_shapes=scratch,
        compiler_params=pltpu.CompilerParams(vmem_limit_bytes=(mib << 20) + 5 * size // 4),
        cost_estimate=pl.CostEstimate(
            flops=int(micros * 1.0e9), bytes_accessed=1 << 20 if micros else 0, transcendentals=0
        ),
    )(*args)


def iota(shape, axis):
    return lax.broadcasted_iota(jnp.int32, shape, axis)


def ones_where(ok, value=1.0):
    return jnp.where(ok, value, 0.0).astype(BF)


def pool_matrix(n, side):
    r, c = iota((n, n), 0), iota((n, n), 1)
    area = side * side
    near_w = jnp.abs(r % side - c % side) <= 1
    near_h = jnp.abs((r // side) % side - (c // side) % side) <= 1
    return ones_where((r // area == c // area) & near_w & near_h)


def turn_matrix(n, area):
    r, c = iota((n, n), 0), iota((n, n), 1)
    return ones_where((r // area == c // area) & (r % area + c % area == area - 1))


def two_matrix(transposed):
    shape = (256, 64) if transposed else (64, 256)
    big, small = (iota(shape, 0), iota(shape, 1)) if transposed else (iota(shape, 1), iota(shape, 0))
    ok = (small // 16 == big // 64) & ((small // 4) % 4 == (big // 16) % 4)
    return ones_where(ok & (small % 4 == (big // 2) % 4), 0.125)


def exact(matrix, values):
    high = values.astype(BF)
    low = (values - high.astype(F32)).astype(BF)
    return mm(matrix, high) + mm(matrix, low)


def own_columns(place, transposed=False):
    shape = (256, LAYER) if transposed else (LAYER, 256)
    lane, col = (iota(shape, 0), iota(shape, 1)) if transposed else (iota(shape, 1), iota(shape, 0))
    wide = (lane < 80) & (col == B0 + 80 * place + lane)
    narrow = (lane >= 80) & (lane < 112) & (col == B0 + B1 + 32 * place + lane - 80)
    at = lane - 128 - POOL_LANE
    pool = (at >= 0) & (at < 32) & (col == B0 + OUTER + 32 * place + at)
    return ones_where(wide | narrow | pool)


def scaled_of(values, sums, voxels):
    centre = sums[0:1] * (1.0 / voxels)
    spread = lax.rsqrt(sums[1:2] * (1.0 / voxels) - centre * centre + EPS)
    return (values - centre) * spread, spread


def normed(values, sums, norms, voxels):
    scaled, _ = scaled_of(values, sums, voxels)
    return scaled, scaled * norms[0:1] + norms[1:2]


def silu(y):
    return y * lax.logistic(y)


def slope(y):
    sigmoid = lax.logistic(y)
    return sigmoid * (1.0 + y * (1.0 - sigmoid))


def norm_back(dy, values, sums, norms, back, voxels):
    scaled, spread = scaled_of(values, sums, voxels)
    scale = norms[0:1] * spread
    return scale * (dy - back[0:1] * (1.0 / voxels) - scaled * (back[1:2] * (1.0 / voxels)))


def add_pair(ref, lanes, first, second):
    ref[0:1, lanes] += jnp.sum(first, 0, keepdims=True)
    ref[1:2, lanes] += jnp.sum(second, 0, keepdims=True)


def shifted(a, side, j, k):
    if j == 0 and k == 0:
        return a
    rows, lanes = a.shape
    area = side * side
    r = iota((area, lanes), 0)
    w, h = r % side + k, r // side + j
    ok = (w >= 0) & (w < side) & (h >= 0) & (h < side)
    moved = pltpu.roll(a, (-(side * j + k)) % rows, 0).reshape(rows // area, area, lanes)
    return jnp.where(ok[None], moved, 0.0).reshape(rows, lanes)


def assemble(me_ref, pieces, buf):
    half = pieces[0].shape[0] // 2
    buf[me_ref[0]] = pieces[0][...]
    for k in range(1, 4):
        place = jnp.bitwise_xor(me_ref[0], k)
        buf[place, pl.ds(pl.multiple_of(half * me_ref[2], half), half), :] = pieces[k][...]
        buf[place, pl.ds(pl.multiple_of(half * (1 - me_ref[2]), half), half), :] = pieces[k + 3][...]


def tap_block(shards, t):
    wide, narrow = [], []
    for w in shards:
        wide.append(w[0:80, B1R * t : B1R * (t + 1)].astype(F32))
        for lane in (B2R * t, NARROW_AT + B2R * t):
            narrow.append(w[80:96, lane : lane + B2R].astype(F32))
    wide = jnp.concatenate(wide, 0)
    narrow = jnp.concatenate(narrow, 0)
    top = jnp.concatenate([wide, jnp.zeros((wide.shape[0], B2R), F32)], 1)
    low = jnp.concatenate([jnp.zeros((narrow.shape[0], B1R), F32), narrow], 1)
    return jnp.concatenate([top, low], 0).astype(BF)


def kernels4_body(me_ref, mine_ref, twin_ref, all_ref, first_ref, last_ref, buf, sems):
    first = pltpu.make_async_copy(all_ref.at[0:9], first_ref, sems.at[0])
    last = pltpu.make_async_copy(all_ref.at[18:27], last_ref, sems.at[1])
    buf[:, pl.ds(pl.multiple_of(48 * me_ref[2], 16), 48), :] = mine_ref[:, :48, :]
    buf[:, pl.ds(pl.multiple_of(48 * (1 - me_ref[2]), 16), 48), :] = twin_ref[:, :48, :]
    for t in range(TAPS):
        all_ref[t] = tap_block([buf.at[z] for z in range(4)], t)
        if t == 8:
            first.start()
    last.start()
    first.wait()
    last.wait()


def kernels5_body(w_ref, all_ref):
    for t in range(TAPS):
        all_ref[t] = jnp.concatenate([tap_block([w_ref], t), jnp.zeros((16, INNER), BF)], 0)


def front_parts(buf, matrix_ref, norms_ref):
    for z in range(4):
        matrix_ref[32 * z : 32 * (z + 1), :] = buf[z, 112:144, :]
        matrix_ref[BP + 112 * z : BP + 112 * (z + 1), :] = buf[z, 0:112, :]
        row = buf[z, 144:160, :].astype(F32)[0:1]
        norms_ref[0:1, 256 * z : 256 * (z + 1)] = row[:, :256]
        norms_ref[1:2, 256 * z : 256 * (z + 1)] = row[:, 256:512]


def total_of(parts):
    return (parts[0][...] + parts[1][...]) + (parts[2][...] + parts[3][...])


def front5_body(me_ref, mine_ref, twin_ref, w_ref, n_ref, own_ref, buf):
    for src, odd in ((mine_ref, me_ref[2]), (twin_ref, 1 - me_ref[2])):
        for j in range(5):
            rows = pl.ds(pl.multiple_of(80 * odd + 16 * j, 16), 16)
            buf[:, rows, :] = src[:, 48:64, LAYER * j : LAYER * (j + 1)]
    front_parts(buf, w_ref, n_ref)
    norms = n_ref[...]
    own = jnp.zeros((2, 256), F32)
    gap = jnp.zeros((2, 16 + POOL_LANE), F32)
    for z in range(4):
        wide = norms[:, REDUCED + 80 * z : REDUCED + 80 * (z + 1)]
        narrow = norms[:, REDUCED + B1 + 32 * z : REDUCED + B1 + 32 * (z + 1)]
        pool = norms[:, REDUCED + OUTER + 32 * z : REDUCED + OUTER + 32 * (z + 1)]
        block = jnp.concatenate([wide, narrow, gap, pool, jnp.zeros((2, 32), F32)], 1)
        own = jnp.where(me_ref[0] == z, block, own)
    own_ref[...] = own


def front4_body(me_ref, x_ref, p0, p1, p2, p3, t1, t2, t3, z_ref, m_ref, w_ref, nf_ref, nb_ref, buf, n_ref):
    assemble(me_ref, (p0, p1, p2, p3, t1, t2, t3), buf)
    front_parts(buf, w_ref, n_ref)
    nf_ref[...] = n_ref[:, :REDUCED]
    nb_ref[:, :BP] = n_ref[:, REDUCED + OUTER :]
    nb_ref[:, BP:] = n_ref[:, REDUCED : REDUCED + OUTER]
    m_ref[...] = jnp.zeros_like(m_ref)
    for f in range(2):
        for h in range(2):
            x = x_ref[4 * h : 4 * h + 4, f].reshape(256, x_ref.shape[3])
            z = mm(x, w_ref[...], NT)
            rows = slice(256 * h, 256 * h + 256)
            z_ref[f, rows, :] = z
            front = z[:, BP:]
            add_pair(m_ref, slice(None), front, front * front)


def act4_body(z_ref, s0, s1, s2, s3, n_ref, a_ref, rim_ref, s_ref, *, voxels):
    s_ref[...] = total_of((s0, s1, s2, s3))
    sums, norms = s_ref[:, B0:], n_ref[:, B0:]
    for f in range(2):
        for h in range(2):
            rows = slice(256 * h, 256 * h + 256)
            _, y = normed(z_ref[f, rows, BP + B0 :], sums, norms, voxels)
            a_ref[f, rows, :] = silu(y).astype(BF)
            rim_ref[f, rows, :BP] = z_ref[f, rows, :BP].astype(BF)
            rim_ref[f, rows, BP:] = silu(y).astype(BF)


def pool4_body(pp_ref, before_ref, after_ref, pool_ref, m_ref):
    matrix = pool_matrix(256, 8)
    m_ref[...] = jnp.zeros_like(m_ref)
    for f in range(2):
        for h in range(2):
            rows = slice(256 * h, 256 * h + 256)
            rim = before_ref if f == 0 else after_ref
            v = pp_ref[0, rows, :BP].astype(F32) + pp_ref[1, rows, :BP].astype(F32)
            v = (v + rim[rows, :BP].astype(F32)).astype(BF)
            out = mm(matrix, v) * (1.0 / 27.0)
            pool_ref[f, rows, :] = out
            add_pair(m_ref, slice(None), out, out * out)


def moments_body(c_ref, p_ref, m_ref):
    m_ref[:, 0:BP] = p_ref[...]
    m_ref[:, BP:] = jnp.zeros((2, OUTER), F32)
    for f in range(2):
        for h in range(2):
            c = c_ref[f, 256 * h : 256 * h + 256, :]
            add_pair(m_ref, slice(BP, None), c, c * c)


def norm4_body(
    z_ref, c_ref, p_ref, sf_ref, s0, s1, s2, s3, nf_ref, nb_ref, w_ref, mid_ref, z5_ref, m_ref, sb_ref, *, voxels
):
    sb_ref[...] = total_of((s0, s1, s2, s3))
    matrix = two_matrix(False)
    sf, sb, nf, nb = sf_ref[:, :B0], sb_ref[...], nf_ref[:, :B0], nb_ref[...]
    for h in range(2):
        rows, outs = slice(256 * h, 256 * h + 256), slice(64 * h, 64 * h + 64)
        pool = direct = conv = 0.0
        for f in range(2):
            pool += silu(normed(p_ref[f, rows, :], sb[:, :BP], nb[:, :BP], voxels)[1])
            direct += silu(normed(z_ref[f, rows, BP : BP + B0], sf, nf, voxels)[1])
            conv += silu(normed(c_ref[f, rows, :], sb[:, BP:], nb[:, BP:], voxels)[1])
        mid_ref[outs, :BP] = exact(matrix, pool).astype(BF)
        mid_ref[outs, BP : BP + B0] = exact(matrix, direct).astype(BF)
        mid_ref[outs, BP + B0 :] = exact(matrix, conv).astype(BF)
    z5 = mm(mid_ref[...], w_ref[...], NT)
    z5_ref[...] = z5
    m_ref[...] = jnp.zeros_like(m_ref)
    add_pair(m_ref, slice(None), z5[:, BP:], z5[:, BP:] * z5[:, BP:])


def act5_body(me_ref, z_ref, s0, s1, s2, s3, n_ref, send_ref, s_ref, *, voxels):
    s_ref[...] = total_of((s0, s1, s2, s3))
    _, y = normed(z_ref[:, BP + B0 :], s_ref[:, B0:], n_ref[:, B0:REDUCED], voxels)
    base = jnp.concatenate([silu(y), jnp.zeros((y.shape[0], 64), F32)], 1)
    pre = z_ref[:, :BP].astype(BF)
    c, lane = iota((BP, 256), 0), iota((BP, 256), 1)
    at = lane - 128 - POOL_LANE
    for k in range(4):
        place = jnp.bitwise_xor(me_ref[0], k)
        pick = ones_where((at >= 0) & (at < 32) & (c == 32 * place + at))
        send_ref[k] = (base + mm(pre, pick)).astype(BF)


def join5_body(me_ref, r0, r1, r2, r3, a_ref, pool_ref, pre):
    pre[0] = jnp.zeros((128, 128), F32)
    pre[5] = jnp.zeros((128, 128), F32)
    for k, r in enumerate((r0, r1, r2, r3)):
        place = jnp.bitwise_xor(me_ref[0], k)
        a_ref[place] = r[:, :INNER]
        pre[place + 1] = r[:, 128:].astype(F32)
    matrix = pool_matrix(128, 4)
    lane = iota((128, 128), 1)
    ok = (lane >= POOL_LANE) & (lane < POOL_LANE + 32)
    for f in range(4):
        v = (pre[f] + pre[f + 1] + pre[f + 2]).astype(BF)
        pool_ref[f] = jnp.where(ok, mm(matrix, v) * (1.0 / 27.0), 0.0)


def moments5_body(c_ref, p_ref, m_ref):
    m_ref[...] = jnp.zeros_like(m_ref)
    for f in range(4):
        c, p = c_ref[f], p_ref[f]
        add_pair(m_ref, slice(0, 128), c, c * c)
        add_pair(m_ref, slice(128, 256), p, p * p)


def cot5_body(me_ref, cot_ref, out_ref):
    for k in range(4):
        pick = own_columns(jnp.bitwise_xor(me_ref[0], k))
        out_ref[k] = mm(cot_ref[...], pick).astype(BF)


def norm5_body(me_ref, c_ref, p_ref, s_ref, n_ref, g0, g1, g2, g3, feat_ref, dy_ref, x_ref, *, voxels):
    x_ref[...] = jnp.zeros_like(x_ref)
    for k, g in enumerate((g0, g1, g2, g3)):
        place = jnp.bitwise_xor(me_ref[0], k)
        for src, lanes in ((c_ref, slice(0, 128)), (p_ref, slice(128, 256))):
            scaled, y = normed(src[place], s_ref[:, lanes], n_ref[:, lanes], voxels)
            sigmoid = lax.logistic(y)
            feat_ref[k, :, lanes] = (y * sigmoid).astype(BF)
            dy = g[:, lanes].astype(F32) * (sigmoid * (1.0 + y * (1.0 - sigmoid)))
            dy_ref[place, :, lanes] = dy
            add_pair(x_ref, lanes, dy, dy * scaled)


def back5_body(c_ref, p_ref, s_ref, n_ref, dy_ref, b_ref, dv_ref, turned_ref, u_ref, *, voxels):
    matrix, turn = pool_matrix(128, 4), turn_matrix(128, 16)
    parts = []
    for f in range(4):
        for src, lanes in ((c_ref, slice(0, 128)), (p_ref, slice(128, 256))):
            dv = norm_back(
                dy_ref[f, :, lanes], src[f], s_ref[:, lanes], n_ref[:, lanes], b_ref[:, lanes],
                voxels,
            )
            if src is c_ref:
                dv_ref[f] = dv.astype(BF)
                turned_ref[3 - f] = mm(turn, dv.astype(BF)).astype(BF)
            else:
                parts.append(dv.astype(BF).astype(F32))
    for f in range(4):
        v = sum(parts[max(f - 1, 0) : f + 2]).astype(BF)
        u_ref[f] = mm(matrix, v) * (1.0 / 27.0)


def send5_body(me_ref, part_ref, u_ref, send_ref):
    turn = turn_matrix(128, 16)
    for k in range(4):
        place = jnp.bitwise_xor(me_ref[0], k)
        part = mm(turn, part_ref[3 - place].astype(BF))
        send_ref[k, :, :128] = part[:, :128].astype(BF)
        tail = jnp.concatenate([part[:, 128:], jnp.zeros((128, 64), F32)], 1)
        send_ref[k, :, 128:] = (tail + u_ref[place]).astype(BF)


def front_back5_body(me_ref, r0, r1, r2, r3, z_ref, s_ref, n_ref, cot_ref, b_ref, dy_ref, u_ref, x_ref, *, voxels):
    x_ref[...] = jnp.zeros_like(x_ref)
    inner = 0.0
    u = 0.0
    c, lane = iota((128, BP), 0) - POOL_LANE, iota((128, BP), 1)
    for k, r in enumerate((r0, r1, r2, r3)):
        place = jnp.bitwise_xor(me_ref[0], k)
        inner = inner + r[:, :INNER].astype(F32)
        u = u + mm(r[:, 128:], ones_where((c >= 0) & (c < 32) & (lane == 32 * place + c)))
    u_ref[...] = u.astype(BF)
    for lanes, grad in ((slice(0, B0), cot_ref[...].astype(F32)), (slice(B0, REDUCED), inner)):
        at = slice(BP + lanes.start, BP + lanes.stop)
        scaled, y = normed(z_ref[:, at], s_ref[:, lanes], n_ref[:, lanes], voxels)
        dy = grad * slope(y)
        dy_ref[:, lanes] = dy
        add_pair(x_ref, lanes, dy, dy * scaled)
    first = jnp.where(me_ref[1] == 0, 1.0, 0.0)
    x_ref[:, pl.ds(pl.multiple_of(512 + 256 * me_ref[0], 128), 256)] = b_ref[...] * first


def mid_back_body(
    dy_ref, z_ref, s_ref, n_ref, b0, b1, b2, b3, u_ref, w_ref, c_ref, p_ref, sb_ref, nb_ref,
    g_ref, gm_ref, x_ref, back_ref, *, voxels,
):
    back_ref[...] = total_of((b0, b1, b2, b3))
    g_ref[:, :BP] = u_ref[...]
    g_ref[:, BP:] = norm_back(
        dy_ref[...], z_ref[:, BP:], s_ref[...], n_ref[:, :REDUCED], back_ref[:, :REDUCED], voxels / 8
    ).astype(BF)
    gm = mm(g_ref[...], w_ref[...])
    gm_ref[...] = gm
    matrix = two_matrix(True)
    x_ref[...] = jnp.zeros_like(x_ref)
    for h in range(2):
        rows = slice(256 * h, 256 * h + 256)
        block = gm[64 * h : 64 * h + 64]
        for src, lanes, at in (
            (p_ref, slice(0, BP), slice(0, BP)),
            (c_ref, slice(BP, BP + OUTER), slice(BP + B0, LAYER)),
        ):
            up = exact(matrix, block[:, at])
            for f in range(2):
                scaled, y = normed(src[f, rows, :], sb_ref[:, lanes], nb_ref[:, lanes], voxels)
                dy = up * slope(y)
                add_pair(x_ref, lanes, dy, dy * scaled)


def front_rows(total, out_ref):
    gap = jnp.zeros((4, total.shape[1]), F32)
    for z in range(4):
        for q in range(4):
            entry, pool = BP + 112 * z + 28 * q, 32 * z + 8 * q
            block = [total[entry : entry + 28], gap, total[pool : pool + 8]]
            out_ref[q, z] = jnp.concatenate(block, 0).astype(BF)


def front_grad5_body(g_ref, mid_ref, out_ref):
    turned = g_ref[...].astype(F32).T.astype(BF)
    front_rows(mm(turned, mid_ref[...]), out_ref)


def branch_grad4_body(
    gm_ref, c_ref, p_ref, s_ref, n_ref, b0, b1, b2, b3, dv_ref, dp_ref, turned_ref, b_ref, *, voxels
):
    turn = turn_matrix(256, 64)
    b_ref[...] = total_of((b0, b1, b2, b3))
    matrix = two_matrix(True)
    for h in range(2):
        rows = slice(256 * h, 256 * h + 256)
        block = gm_ref[64 * h : 64 * h + 64, :]
        for src, dst, lanes, at in (
            (p_ref, dp_ref, slice(0, BP), slice(0, BP)),
            (c_ref, dv_ref, slice(BP, BP + OUTER), slice(BP + B0, LAYER)),
        ):
            up = exact(matrix, block[:, at])
            sums, norms, back = s_ref[:, lanes], n_ref[:, lanes], b_ref[:, lanes]
            for f in range(2):
                values = src[f, rows, :]
                _, y = normed(values, sums, norms, voxels)
                dv = norm_back(up * slope(y), values, sums, norms, back, voxels)
                dst[f, rows, :] = dv.astype(BF)
                if dst is dv_ref:
                    turned_ref[1 - f, rows, :] = mm(turn, dv.astype(BF)).astype(BF)


def put(out_ref, place, rows, lane, value):
    size = out_ref.shape[-1]
    done, width = 0, value.shape[1]
    while done < width:
        part, at = divmod(lane + done, size)
        step = min(width - done, size - at)
        out_ref[part, place, rows, at : at + step] = value[:, done : done + step].astype(BF)
        done += step


def taps_out(out_ref, t, grad, slots):
    places = len(slots)
    for z, slot in enumerate(slots):
        put(out_ref, slot, slice(0, 80), B1R * t, grad[80 * z : 80 * z + 80, :B1R])
        low = grad[80 * places + 32 * z : 80 * places + 32 * z + 32, B1R:INNER]
        put(out_ref, slot, slice(80, 96), B2R * t, low[:16])
        put(out_ref, slot, slice(80, 96), NARROW_AT + B2R * t, low[16:])


def wide_lanes(a):
    return jnp.concatenate([a.astype(F32), jnp.zeros((a.shape[0], 64), F32)], 1)


def kernel_grad4_body(me_ref, a_ref, before_ref, after_ref, dv_ref, out_ref, patches, turned):
    out_ref[...] = jnp.zeros_like(out_ref)
    slots = [jnp.bitwise_xor(me_ref[0], z) for z in range(4)]
    for f in range(2):
        turned[:, 512 * f : 512 * f + 512] = dv_ref[f].astype(F32).T.astype(BF)
    for n in range(9):
        for q in range(4):
            a = before_ref[...] if q == 0 else after_ref[...] if q == 3 else a_ref[q - 1]
            patches[n % 2, q] = shifted(wide_lanes(a), 8, n // 3 - 1, n % 3 - 1).astype(BF)
        for i in range(3):
            window = patches[n % 2, i : i + 2].reshape(1024, 256)
            taps_out(out_ref, 9 * i + n, mm(turned[...], window), slots)


def kernel_grad5_body(a_ref, dv_ref, out_ref, patches, turned):
    out_ref[...] = jnp.zeros_like(out_ref)
    for q in (0, 5):
        patches[q] = jnp.zeros(patches.shape[1:], BF)
    for q in range(4):
        a = wide_lanes(a_ref[q])
        for n in range(9):
            patches[q + 1, :, 256 * n : 256 * n + 256] = shifted(a, 4, n // 3 - 1, n % 3 - 1).astype(BF)
        turned[:, 128 * q : 128 * q + 128] = dv_ref[q].astype(F32).T.astype(BF)
    for t in range(TAPS):
        i, n = t // 9, t % 9
        window = patches[i : i + 4, :, 256 * n : 256 * n + 256].reshape(512, 256)
        taps_out(out_ref, t, mm(turned[...], window), [0])


def front_back4_body(
    gm_ref, z_ref, s_ref, n_ref, own_ref, before_ref, after_ref, dp_ref, dy_ref, u_ref, x_ref, *, voxels
):
    two, pool, turn = two_matrix(True), pool_matrix(256, 8), turn_matrix(256, 64)
    x_ref[...] = jnp.zeros_like(x_ref)
    for h in range(2):
        rows = slice(256 * h, 256 * h + 256)
        up = exact(two, gm_ref[64 * h : 64 * h + 64, BP : BP + B0])
        for f in range(2):
            rim = before_ref if f == 0 else after_ref
            v = dp_ref[0, rows, :].astype(F32) + dp_ref[1, rows, :].astype(F32)
            v = (v + rim[rows, :BP].astype(F32)).astype(BF)
            u_ref[f, rows, :] = (mm(pool, v) * (1.0 / 27.0)).astype(BF)
            inner = exact(turn, own_ref[1 - f, rows, :] + rim[rows, BP:].astype(F32))
            for lanes, grad in ((slice(0, B0), up), (slice(B0, REDUCED), inner)):
                at = slice(BP + lanes.start, BP + lanes.stop)
                scaled, y = normed(z_ref[f, rows, at], s_ref[:, lanes], n_ref[:, lanes], voxels)
                dy = grad * slope(y)
                dy_ref[f, rows, lanes] = dy
                add_pair(x_ref, lanes, dy, dy * scaled)


def front_grad4_body(z_ref, s_ref, n_ref, dy_ref, b0, b1, b2, b3, u_ref, x_ref, g_ref, out_ref, b_ref, *, voxels):
    b_ref[...] = total_of((b0, b1, b2, b3))
    total = 0.0
    for f in range(2):
        for h in range(2):
            rows = slice(256 * h, 256 * h + 256)
            g_ref[f, rows, :BP] = u_ref[f, rows, :]
            g_ref[f, rows, BP:] = norm_back(
                dy_ref[f, rows, :], z_ref[f, rows, BP:], s_ref[...], n_ref[...], b_ref[...], voxels
            ).astype(BF)
        turned = g_ref[f].astype(F32).T.astype(BF)
        total = total + mm(turned, x_ref[:, f].reshape(512, x_ref.shape[3]))
    front_rows(total, out_ref)


def clips_grad_body(g_ref, w_ref, out_ref):
    for f in range(2):
        for h in range(2):
            grad = mm(g_ref[f, 256 * h : 256 * h + 256, :], w_ref[...])
            out_ref[4 * h : 4 * h + 4, f] = grad.reshape(4, 64, out_ref.shape[3])


def lines(buf, first, count, starts, width):
    out = []
    for r in range(4):
        rows = pl.ds(first + r, count, stride=4)
        part = []
        for at in starts:
            tiles = [buf[at + n, rows, :] for n in range(-(-width // 128))]
            part.append(jnp.concatenate(tiles, 1)[:, :width])
        out.append(jnp.concatenate(part, 0) if len(part) > 1 else part[0])
    return jnp.concatenate(out, 1)


def rows_body(me_ref, mine_ref, twin_ref, wide_ref, narrow_ref, buf):
    wide, narrow = [], []
    for t in range(2):
        for q in range(4):
            same = me_ref[2] == q % 2
            for n in range(9):
                lanes = slice(128 * n, 128 * (n + 1))
                mine, twin = mine_ref[t, q // 2, :, lanes], twin_ref[t, q // 2, :, lanes]
                buf[9 * q + n] = jnp.where(same, mine.astype(F32), twin.astype(F32))
        wide.append(lines(buf, 0, 20, (0,), TAPS * B1R))
        narrow.append(lines(buf, 80, 4, (0, NARROW_AT // 128), TAPS * B2R))
    for pair, out_ref in ((wide, wide_ref), (narrow, narrow_ref)):
        count, size = pair[0].shape
        for n in range(count):
            rows = [part[n : n + 1] for part in pair]
            out_ref[:, size * n : size * (n + 1)] = jnp.concatenate(rows, 0)


def fronts_body(both_ref, entry4_ref, pool4_ref, entry5_ref, pool5_ref):
    for q in range(4):
        pair = [both_ref[t, q].astype(F32) for t in range(2)]
        for lanes, entry_ref, pool_ref in (
            (slice(0, 528), entry4_ref, pool4_ref),
            (slice(576, 1408), entry5_ref, pool5_ref),
        ):
            size = lanes.stop - lanes.start
            for n in range(36):
                row = n if n < 28 else n + 4
                value = jnp.concatenate([p[row : row + 1, lanes] for p in pair], 0)
                at = 28 * q + n if n < 28 else 8 * q + n - 28
                (entry_ref if n < 28 else pool_ref)[:, size * at : size * (at + 1)] = value


def features_body(me_ref, z_ref, s_ref, n_ref, r0, r1, r2, r3, out_ref, *, voxels):
    rest = 0.0
    for k, r in enumerate((r0, r1, r2, r3)):
        rest = rest + mm(r[...], own_columns(jnp.bitwise_xor(me_ref[0], k), True))
    _, y = normed(z_ref[:, BP : BP + B0], s_ref[:, :B0], n_ref[:, :B0], voxels)
    out_ref[:, :B0] = silu(y)
    out_ref[:, B0:] = rest[:, B0:]


def xor_pairs(axis, step):
    return [(i, i ^ step) for i in range(lax.axis_size(axis))]


def tower_steps():
    steps, step = [], 1
    while step < lax.axis_size("dp") // 2:
        steps.append(step)
        step *= 2
    return steps


def other_tower(value):
    return lax.ppermute(value, "dp", xor_pairs("dp", lax.axis_size("dp") // 2))


def blk_peers(value):
    count = lax.axis_size("blk")
    return [value] + [lax.ppermute(value, "blk", xor_pairs("blk", k)) for k in range(1, count)]


def by_place(parts):
    me, step = lax.axis_index("blk"), 1
    while step < len(parts):
        hit = (me & step) != 0
        parts = [jnp.where(hit, parts[k ^ step], parts[k]) for k in range(len(parts))]
        step *= 2
    return parts


def swap_blk(mine):
    return [mine[0]] + [
        lax.ppermute(mine[k], "blk", xor_pairs("blk", k)) for k in range(1, lax.axis_size("blk"))
    ]


def dp_sum(value):
    for step in tower_steps():
        value = value + lax.ppermute(value, "dp", xor_pairs("dp", step))
    return value


def tower_parts(value):
    return blk_peers(dp_sum(value))


def gather_pieces(shard):
    rows = shard.shape[0] // 2
    odd = lax.axis_index("dp") % 2
    half = lax.dynamic_slice_in_dim(shard, odd * rows, rows, 0)
    mine = blk_peers(half)[1:]
    twins = [lax.ppermute(piece, "dp", xor_pairs("dp", 1)) for piece in mine]
    return [shard] + mine + twins


def fours():
    return [list(range(i, i + 4)) for i in range(0, lax.axis_size("dp"), 4)]


def scatter_four(value):
    value = lax.psum_scatter(
        value, "dp", scatter_dimension=0, axis_index_groups=fours(), tiled=False
    )
    for step in tower_steps()[2:]:
        got = lax.ppermute(value, "dp", xor_pairs("dp", step))
        value = (value.astype(F32) + got.astype(F32)).astype(BF)
    return value


def gather_eight(value):
    half = lax.axis_size("dp") // 2
    groups = [
        [b + i for i in range(4)] + [half + b + i for i in range(4)] for b in range(0, half, 4)
    ]
    return lax.all_gather(value, "dp", axis_index_groups=groups, tiled=False)


def after(values, first):
    values, _ = lax.optimization_barrier((values, first))
    return values


def rim_swap(first, last):
    count = lax.axis_size("blk")
    ahead = [(i, i + 1) for i in range(count - 1)]
    back = [(i + 1, i) for i in range(count - 1)]
    return lax.ppermute(last, "blk", ahead), lax.ppermute(first, "blk", back)


def step_rows(value, axis, step, first=None):
    if step in tower_steps()[:2]:
        rows = value.shape[axis] // 2
        high = (lax.axis_index("dp") & step) != 0
        keep = lax.dynamic_slice_in_dim(value, jnp.where(high, rows, 0), rows, axis)
        give = lax.dynamic_slice_in_dim(value, jnp.where(high, 0, rows), rows, axis)
    else:
        keep = give = value
    got = lax.ppermute(give, "dp", xor_pairs("dp", step))
    if first is not None:
        got = after(got, first)
    return (keep.astype(F32) + got.astype(F32)).astype(BF)


def reduce_rows(value, axis, steps=None):
    for step in tower_steps() if steps is None else steps:
        value = step_rows(value, axis, step)
    return value


def reduce_blk(value):
    count = value.shape[0]
    got = swap_blk(by_place([value[j] for j in range(count)]))
    total = got[0].astype(F32)
    for piece in got[1:]:
        total = total + piece.astype(F32)
    return total.astype(BF)


def spread_rows(value):
    stream = lax.axis_index("dp") // (lax.axis_size("dp") // 2)
    other = other_tower(value)
    both = jnp.where(stream == 0, jnp.stack([value, other]), jnp.stack([other, value]))
    for step in (2, 1):
        got = lax.ppermute(both, "dp", xor_pairs("dp", step))
        high = (lax.axis_index("dp") & step) != 0
        both = jnp.where(
            high, jnp.concatenate([got, both], 1), jnp.concatenate([both, got], 1)
        )
    return both


def branch_rows(me, mine, twin):
    return call(
        rows_body,
        (shape_of((2, 80 * TAPS * B1R)), shape_of((2, 32 * TAPS * B2R))),
        me, mine, twin,
        micros=3, mib=16, scratch=[pltpu.VMEM((36, 96, 128), F32)],
    )


def pick_row(param, stream):
    size = param.shape[1]
    return lax.dynamic_index_in_dim(param.reshape(2, size // 128, 128), stream, 0, keepdims=False)


def on_device(clips, cotangent, *params):
    groups = lax.axis_size("dp")
    count = lax.axis_size("blk")
    stream = lax.axis_index("dp") // (groups // 2)
    place = lax.axis_index("blk")
    index = lax.axis_index("dp")
    me = jnp.stack([place, index % (groups // 2), index % 2, index // 2 % 2]).astype(jnp.int32)
    own = [pick_row(p, stream) for p in params]
    early, late = own[:6], own[6:]
    n, frames, height, breadth, c_first = clips.shape
    voxels = groups // 2 * count * n * frames * height * breadth
    late_voxels = voxels // 8
    x = clips.reshape(n, frames, height * breadth, c_first)
    e, p = REDUCED // count, BP // count
    g = (REDUCED + OUTER + BP) // count

    def pack_front(layer, c, turn=0):
        norms = jnp.concatenate([layer[4].reshape(-1), layer[5].reshape(-1)])
        row = jnp.pad(norms, (0, c - 2 * g)).reshape(1, c)
        rows = jnp.concatenate([layer[0].reshape(e, c), layer[3].reshape(p, c)])
        if turn:
            rows = jnp.concatenate([rows[:, c - turn :], rows[:, : c - turn]], 1)
        return jnp.pad(jnp.concatenate([rows, row]), ((0, 160 - e - p - 1), (0, 0)))

    def pack_branch(layer):
        wide = layer[1].reshape(80, -1)
        narrow = layer[2].reshape(32, -1)
        gap = jnp.zeros((16, NARROW_AT - narrow.shape[1]), BF)
        low = jnp.concatenate([narrow[:16], gap, narrow[16:]], 1)
        low = jnp.pad(low, ((0, 0), (0, wide.shape[1] - low.shape[1])))
        return jnp.concatenate([wide, low])

    packed = lax.dynamic_slice_in_dim(pack_branch(early), index % 2 * 48, 48, 0)
    pieces = gather_pieces(pack_front(after(early, packed), c_first))
    late_front = lax.dynamic_slice_in_dim(pack_front(late, LAYER, BP), index % 2 * 80, 80, 0)
    late_front = late_front.reshape(5, 16, LAYER).transpose(1, 0, 2).reshape(16, 5 * LAYER)
    late_front = jnp.pad(late_front, ((0, 0), (0, packed.shape[1] - 5 * LAYER)))
    packed = jnp.concatenate([packed, late_front])
    packed = lax.all_gather(packed, "blk", tiled=False)
    late = after(late, pieces[0])
    taps_5 = call(kernels5_body, shape_of((TAPS, 128, INNER), BF), pack_branch(late), micros=2)
    x = after(x, taps_5)
    z, m, front_4, nf4, nb4 = call(
        front4_body,
        (
            shape_of((2, 512, 576)), shape_of((2, REDUCED)), shape_of((576, c_first), BF),
            shape_of((2, REDUCED)), shape_of((2, 576)),
        ),
        me, x, *pieces, micros=0,
        scratch=[pltpu.VMEM((4, 160, c_first), BF), pltpu.VMEM((2, 1024), F32)],
    )
    late, cotangent = after((late, cotangent), m)
    cot = cotangent.reshape(128, LAYER)
    cot_mine = call(cot5_body, shape_of((4, 128, 256), BF), me, cot, micros=2)

    def conv(values, kernel, pads, order):
        return lax.conv_general_dilated(
            values,
            kernel.reshape(-1, 3, 3, *kernel.shape[1:]),
            (1, 1, 1),
            pads,
            dimension_numbers=("DNHWC", order, "DNHWC"),
            preferred_element_type=F32,
        )

    forth, back = "DHWOI", "DHWIO"
    flat_pads = ((0, 0), (1, 1), (1, 1))
    same = ((1, 1), (1, 1), (1, 1))
    at4 = functools.partial(functools.partial, voxels=voxels)
    at5 = functools.partial(functools.partial, voxels=late_voxels)

    parts = tower_parts(m)
    z_then = after(z, cot_mine)
    a, rims, sf4 = call(
        at4(act4_body),
        (shape_of((2, 512, INNER), BF), shape_of((2, 512, BP + INNER), BF), shape_of((2, REDUCED))),
        z_then, *parts, nf4, micros=0,
    )
    before, behind = rim_swap(rims[0], rims[1])
    packed = after(packed, a)
    twin = lax.ppermute(packed, "dp", xor_pairs("dp", 1))
    taps_4, taps_first, taps_last = call(
        kernels4_body,
        (
            shape_of((TAPS, OUTER, INNER), BF),
            shape_of((9, OUTER, INNER), BF), shape_of((9, OUTER, INNER), BF),
        ),
        me, packed, twin, micros=5, mib=12, away=(1, 2),
        scratch=[pltpu.VMEM((4, 96, 4320), BF), pltpu.SemaphoreType.DMA((2,))],
    )
    before, behind = after((before, behind), taps_4)
    pool, m_pool = call(
        pool4_body, (shape_of((2, 512, BP)), shape_of((2, BP))), rims, before, behind, micros=2
    )
    before, behind = before[:, BP:], behind[:, BP:]
    a_pad = jnp.concatenate([before[None], a, behind[None]]).reshape(4, n, height, breadth, INNER)
    c = conv(a_pad, taps_4, flat_pads, forth).reshape(2, 512, OUTER)
    front_5, n5f, n5 = call(
        front5_body,
        (shape_of((576, LAYER), BF), shape_of((2, 1024)), shape_of((2, 256))),
        me, packed, twin, micros=1, scratch=[pltpu.VMEM((4, 160, LAYER), BF)],
    )
    cots = swap_blk([after(cot_mine, c)[k] for k in range(4)])
    parts = tower_parts(call(moments_body, shape_of((2, 576)), c, m_pool, micros=1))

    mid, z5, m, sb4 = call(
        at4(norm4_body),
        (shape_of((128, LAYER), BF), shape_of((128, 576)), shape_of((2, REDUCED)), shape_of((2, 576))),
        z, c, pool, sf4, *parts, nf4, nb4, front_5, micros=4, lazy=(0, 2, 3, 8, 9, 10),
    )
    send, sf5 = call(
        at5(act5_body),
        (shape_of((4, 128, 256), BF), shape_of((2, REDUCED))),
        me, z5, *tower_parts(m), n5f, micros=1,
    )
    a5, pool5 = call(
        join5_body,
        (shape_of((4, 128, INNER), BF), shape_of((4, 128, 128))),
        me, *swap_blk([send[k] for k in range(4)]),
        micros=1, scratch=[pltpu.VMEM((6, 128, 128), F32)],
    )
    small = (4, n, height // 2, breadth // 2, -1)
    c5 = conv(a5.reshape(small), taps_5, same, forth).reshape(4, 128, 128)
    s5 = dp_sum(call(moments5_body, shape_of((2, 256)), c5, pool5, micros=1))
    feat, dy5, m = call(
        at5(norm5_body),
        (shape_of((4, 128, 256), BF), shape_of((4, 128, 256)), shape_of((2, 256))),
        me, c5, pool5, s5, n5, *cots, micros=1, lazy=(2, 4, 5, 6, 7, 8),
    )

    feat = swap_blk([feat[k] for k in range(4)])
    b5 = after(dp_sum(m), feat)
    dv5, turned5, u5 = call(
        at5(back5_body),
        (shape_of((4, 128, 128), BF), shape_of((4, 128, 128), BF), shape_of((4, 128, 128))),
        c5, pool5, s5, n5, dy5, b5, micros=1, lazy=(0, 1, 2, 3, 4),
    )
    part = conv(turned5.reshape(small), taps_5, same, back).reshape(4, 128, INNER)
    send = call(send5_body, shape_of((4, 128, 256), BF), me, part, u5, micros=1)
    dv5 = after(dv5, send)
    got5 = swap_blk([send[k] for k in range(4)])
    branch_part5 = call(
        kernel_grad5_body,
        shape_of((4, 1, 96, 1152), BF),
        a5, dv5,
        micros=2, mib=16,
        scratch=[pltpu.VMEM((6, 128, 2304), BF), pltpu.VMEM((128, 512), BF)],
    )
    z5 = after(z5, branch_part5)
    branch_5 = scatter_four(branch_part5)
    dyf5, u5, m = call(
        at5(front_back5_body),
        (shape_of((128, REDUCED)), shape_of((128, BP), BF), shape_of((2, 1536))),
        me, *got5, z5, sf5, n5f, cot[:, :B0], b5, micros=1,
        lazy=(5, 6, 7, 8, 9),
    )
    parts = tower_parts(m)
    g5, gm, m, back5 = call(
        at4(mid_back_body),
        (shape_of((128, 576), BF), shape_of((128, LAYER)), shape_of((2, 576)), shape_of((2, 1536))),
        dyf5, z5, sf5, n5f, *parts, u5, front_5, c, pool, sb4, nb4, micros=4,
        lazy=(0, 1, 2, 3, 8, 9, 10, 11, 12, 13),
    )

    parts = tower_parts(m)
    front_part5 = call(
        front_grad5_body, shape_of((4, 4, 40, LAYER), BF), after(g5, parts[0]), mid, micros=1
    )
    front_part5 = jnp.concatenate([front_part5[..., BP:], front_part5[..., :BP]], 3)
    front_5_sum = step_rows(front_part5, 0, 1)
    gm = after(gm, front_5_sum)
    both5 = gather_eight(after(branch_5, parts[0])[0]).reshape(2, 4, 96, 1152)
    dv, dp, turned4, bb4 = call(
        at4(branch_grad4_body),
        (
            shape_of((2, 512, OUTER), BF), shape_of((2, 512, BP), BF),
            shape_of((2, 512, OUTER), BF), shape_of((2, 576)),
        ),
        gm, c, pool, sb4, nb4, *parts, micros=3, lazy=(0, 1, 2, 3, 4),
    )
    image = (1, n, height, breadth, OUTER)
    rim_first = conv(turned4[1].reshape(image), taps_first, flat_pads, back).reshape(512, INNER)
    rim_last = conv(turned4[0].reshape(image), taps_last, flat_pads, back).reshape(512, INNER)
    rim_first = jnp.concatenate([dp[0], rim_first.astype(BF)], 1)
    rim_last = jnp.concatenate([dp[1], rim_last.astype(BF)], 1)
    got_before, got_after = rim_swap(rim_first, rim_last)
    branch_part4 = call(
        kernel_grad4_body,
        shape_of((4, 4, 96, 1152), BF),
        me, a, before, behind, after(dv, (rim_first, rim_last)),
        micros=8, mib=10,
        scratch=[pltpu.VMEM((2, 4, 512, 256), BF), pltpu.VMEM((OUTER, 1024), BF)],
    )
    turned4 = after(turned4, (branch_part4, both5))
    branch_part4 = scatter_four(branch_part4)
    front_5_sum = reduce_rows(front_5_sum, 0, tower_steps()[1:])[0]
    inner = conv(turned4.reshape(2, n, height, breadth, OUTER), taps_4, same, back)
    dyf4, u4, m = call(
        at4(front_back4_body),
        (shape_of((2, 512, REDUCED)), shape_of((2, 512, BP), BF), shape_of((2, REDUCED))),
        gm, z, sf4, nf4, inner.reshape(2, 512, INNER), got_before, got_after, dp, micros=4,
        lazy=(0, 1, 2, 3, 5, 6, 7),
    )
    parts = tower_parts(m)
    branch_4 = after(branch_part4, parts[3])
    both5 = both5.reshape(2, 2, 2, 96, 1152)
    wide_5, narrow_5 = branch_rows(jnp.zeros_like(me), both5[:, :, 0], both5[:, :, 1])
    z = after(z, (front_5_sum, wide_5, narrow_5))
    g4, front_part4, bf4 = call(
        at4(front_grad4_body),
        (shape_of((2, 512, 576), BF), shape_of((4, 4, 40, c_first), BF), shape_of((2, REDUCED))),
        z, sf4, nf4, dyf4, *parts, u4, x, micros=4, lazy=(1, 2),
    )
    clips_grad = call(
        clips_grad_body, shape_of((n, frames, height * breadth, c_first)), g4, front_4, micros=3
    )

    norms4 = jnp.concatenate([bf4, bb4[:, BP:], bb4[:, :BP]], 1)
    all5 = back5[:, 512:].reshape(2, count, 256)
    norms5 = jnp.concatenate(
        [
            back5[:, :REDUCED],
            all5[:, :, :80].reshape(2, -1),
            all5[:, :, 80:112].reshape(2, -1),
            all5[:, :, 128 + POOL_LANE : 160 + POOL_LANE].reshape(2, -1),
        ],
        axis=1,
    )
    norms = jnp.stack([norms4, norms5])
    theirs = other_tower(norms)
    fronts = after(step_rows(front_part4, 0, 1), branch_4)
    got = swap_blk([branch_4[k] for k in range(4)])
    fronts = step_rows(fronts, 0, 2, got)
    fronts = reduce_rows(fronts, 0, tower_steps()[2:])[0]
    fronts = jnp.concatenate([fronts, jnp.zeros((4, 40, 48), BF), front_5_sum], 2)
    branch_4 = sum(piece.astype(F32) for piece in got).astype(BF)
    features = call(
        at5(features_body), shape_of((128, LAYER)), me, z5, sf5, n5f, *feat, micros=2
    ).reshape(cotangent.shape)

    side = lax.ppermute(branch_4, "dp", xor_pairs("dp", 2))
    other = other_tower(branch_4)
    fronts = after(fronts, (branch_4, theirs, features, clips_grad))
    norms = jnp.where(stream == 0, jnp.stack([norms, theirs]), jnp.stack([theirs, norms]))
    norms = lax.dynamic_slice_in_dim(norms, place * g, g, 3)
    gains_4, shifts_4, gains_5, shifts_5 = (norms[:, 0, 1], norms[:, 0, 0], norms[:, 1, 1], norms[:, 1, 0])
    got = swap_blk(by_place([fronts[j] for j in range(count)]))
    fronts = sum(piece.astype(F32) for piece in got).astype(BF)
    corner = jnp.concatenate(
        [
            lax.ppermute(other[:48], "dp", xor_pairs("dp", 2)),
            other_tower(side[48:]),
        ]
    )
    corner = after(corner, (gains_4, shifts_4, gains_5, shifts_5))
    right = index // 2 % 2 == 1
    ours = jnp.where(right, jnp.stack([side, branch_4]), jnp.stack([branch_4, side]))
    others = jnp.where(right, jnp.stack([corner, other]), jnp.stack([other, corner]))
    both = jnp.where(stream == 0, jnp.stack([ours, others]), jnp.stack([others, ours]))
    wide_4, narrow_4 = branch_rows(me, both, lax.ppermute(both, "dp", xor_pairs("dp", 1)))
    entry_4, poolproj_4, entry_5, poolproj_5 = call(
        fronts_body,
        (
            shape_of((2, 112 * c_first)), shape_of((2, 32 * c_first)),
            shape_of((2, 112 * LAYER)), shape_of((2, 32 * LAYER)),
        ),
        spread_rows(fronts[None]), micros=2, mib=10,
    )

    return (
        features, clips_grad.reshape(clips.shape),
        entry_4, wide_4, narrow_4, poolproj_4, gains_4, shifts_4,
        entry_5, wide_5, narrow_5, poolproj_5, gains_5, shifts_5,
    )


def solution(mesh):
    spec = P("dp", "blk", None, None, None)
    flat = P(None, "blk")
    return jax.shard_map(
        on_device,
        mesh=mesh,
        in_specs=(spec, spec) + (flat,) * 12,
        out_specs=(spec, spec) + (flat,) * 12,
        check_vma=False,
    )
```

profile of v0, /device:TPU:0, one launch (start us, length us, event | category | flops | bytes accessed | tf_op | source)
XLA Modules:
  0.0 331.7 jit_solution(1377914928450391641)
XLA Ops:
  15.8 5.0 %collective-permute-start.2 = (bf16[80,528]{1,0:T(8,128)(2,1)}, bf16[80,528]{1,0:T(8,128)(2,1)S(1)}, u32[]{:S(2)}, u32[]{:S(2)}) collective-permute-start(bf16[80,528]{1,0:T(8,128)(2,1)} %constant_dynamic-slice_fusion.8), channel_id=1, source_target_pairs={{0,3},{1,2},{2,1},{3,0},{4,7},{5,6},{6,5},{7,4},{8,11},{9,10},{10,... | collective-permute-start | bytes 253448 | tf_op jit(solution)/shard_map/ppermute | solution.py:651
  24.9 9.8 %collective-permute-done.1.p2 = bf16[80,528]{1,0:T(8,128)(2,1)S(1)} collective-permute-done((bf16[80,528]{1,0:T(8,128)(2,1)}, bf16[80,528]{1,0:T(8,128)(2,1)S(1)}, u32[]{:S(2)}, u32[]{:S(2)}) %collective-permute-start.1) | collective-permute-done | bytes 84512 | tf_op jit(solution)/shard_map/ppermute | solution.py:651
  36.4 2.4 shard_map.246
  45.9 4.9 %collective-permute-start.10 = (f32[2,448]{1,0:T(2,128)S(1)}, f32[2,448]{1,0:T(2,128)S(1)}, u32[]{:S(2)}, u32[]{:S(2)}) collective-permute-start(f32[2,448]{1,0:T(2,128)S(1)} %add.158.s0), channel_id=1, source_target_pairs={{0,3},{1,2},{2,1},{3,0},{4,7},{5,6},{6,5},{7,4},{8,11},{9,10},{10,... | collective-permute-start | bytes 10760 | tf_op jit(solution)/shard_map/ppermute | solution.py:651
  55.9 10.7 %all-gather.6.cloned.1.call-done = bf16[256,4320]{1,0:T(8,128)(2,1)} async-done(((bf16[64,4320]{1,0:T(8,128)(2,1)}), bf16[256,4320]{1,0:T(8,128)(2,1)}) %all-gather.6.cloned.1.call-update) | async-done | bytes 2211856 | tf_op jit(solution)/shard_map/all_gather | solution.py:816
  68.5 4.8 %collective-permute-start.11 = (bf16[512,320]{1,0:T(8,128)(2,1)S(1)}, bf16[512,320]{1,0:T(8,128)(2,1)S(1)}, u32[]{:S(2)}, u32[]{:S(2)}) collective-permute-start(bf16[512,320]{1,0:T(8,128)(2,1)S(1)} %get-tuple-element.228), channel_id=1, source_target_pairs={{0,1},{1,2},{2,3},{4,5},{5,6},{6,7},{8,9},{9,10},{10,11},{12,13},{... | collective-permute-start | bytes 983048 | tf_op jit(solution)/shard_map/ppermute | solution.py:719
  73.3 3.0 shard_map.249
  82.4 7.5 %fusion.2 = f32[2,8,8,8,448]{4,1,3,2,0:T(8,128)S(1)} fusion(bf16[3,3,3,448,192]{4,3,2,1,0:T(8,128)(2,1)S(1)} %bitcast.173, bf16[1,8,8,8,192]{4,1,3,2,0:T(8,128)(2,1)S(1)} %copy.66, bf16[2,8,8,8,192]{4,1,3,2,0:T(8,128)(2,1)S(1)} %copy.65, bf16[1,8,8,8,192]{4,1,3,2,0:T(8,128)(2,1)S(1)} %copy.64), kind=kOutput, calls=%fused_computation.11 | convolution fusion | flops 3999006720 | bytes 7266304 | tf_op jit(solution)/shard_map/conv_general_dilated | solution.py:834
  94.3 2.1 collective-permute-done.15
  96.4 2.5 collective-permute-start.18
  104.0 12.7 %shard_map.253 = (bf16[128,832]{1,0:T(8,128)(2,1)S(1)}, f32[128,576]{1,0:T(8,128)S(1)}, f32[2,448]{1,0:T(2,128)S(1)}, f32[2,576]{1,0:T(2,128)S(1)}) custom-call(f32[2,512,576]{2,1,0:T(8,128)S(1)} %copy-done.4, f32[2,512,448]{2,1,0:T(8,128)S(1)} %bitcast.179, f32[2,512,128]{2,1,0:T(8,128)S(1)} %get-tuple-element.114.refs_2_.refs_11_, ...), custom_call_target="tpu_custom_call" | custom-call | flops 4000000000 | bytes 1048576 | tf_op jit(solution)/shard_map/pallas_call | solution.py:68
  119.4 2.1 collective-permute-done.20
  123.5 2.5 collective-permute-start.21
  128.3 2.4 collective-permute-start.26
  132.8 2.4 collective-permute-start.31
  135.5 2.2 collective-permute-start.29
  139.4 2.0 fusion.25
  144.3 2.1 collective-permute-done.28
  147.8 2.2 collective-permute-start.36
  150.0 2.3 collective-permute-start.34
  154.9 2.1 collective-permute-done.33
  160.0 2.3 shard_map.260
  162.4 2.2 collective-permute-start.39
  164.6 2.2 collective-permute-start.37
  174.4 2.2 collective-permute-done.41
  176.6 2.1 collective-permute-start.44
  178.7 2.3 collective-permute-start.42
  183.3 2.6 shard_map.263
  189.3 2.1 collective-permute-done.46
  198.1 2.1 add_convert_fusion
  202.4 2.9 shard_map.266
  211.7 7.8 %shard_map.267 = bf16[4,4,96,1152]{3,2,1,0:T(8,128)(2,1)S(1)} custom-call(s32[4]{0:T(128)S(1)} %pad_add_fusion.me_ref.refs_0_, bf16[2,512,192]{2,1,0:T(8,128)(2,1)S(1)} %copy-done.15, bf16[512,192]{1,0:T(8,128)(2,1)S(1)} %copy-done.13, bf16[512,192]{1,0:T(8,128)(2,1)S(1)} %slice.193.after_ref, bf16[2,512,448]{2,1,0:T(8,128)(2,1)S(1)} %get-tuple-element.156.dv_ref), custom_call_target="tpu_custom_call" | custom-call | flops 8000000000 | bytes 1048576 | tf_op jit(solution)/shard_map/pallas_call | solution.py:68
  223.0 4.6 %collective-permute-start.52 = (bf16[512,320]{1,0:T(8,128)(2,1)}, bf16[512,320]{1,0:T(8,128)(2,1)S(1)}, u32[]{:S(2)}, u32[]{:S(2)}) collective-permute-start(bf16[512,320]{1,0:T(8,128)(2,1)} %pad_maximum_fusion.1), channel_id=1, source_target_pairs={{0,1},{1,2},{2,3},{4,5},{5,6},{6,7},{8,9},{9,10},{10,11},{12,13},{... | collective-permute-start | bytes 983048 | tf_op jit(solution)/shard_map/ppermute | solution.py:719
  229.9 10.5 %fusion.8 = f32[2,8,8,8,192]{4,1,3,2,0:T(8,128)S(1)} fusion(bf16[3,3,3,448,192]{4,3,2,1,0:T(8,128)(2,1)} %bitcast.174, bf16[2,8,8,8,448]{4,3,2,1,0:T(8,128)(2,1)S(1)} %bitcast.169), kind=kOutput, calls=%fused_computation.17 | convolution fusion | flops 2664431616 | bytes 6348800 | tf_op jit(solution)/shard_map/conv_general_dilated | solution.py:834
  241.7 2.6 shard_map.268
  249.4 1.9 collective-permute-done.55
  251.6 2.7 collective-permute-start.57
  257.3 4.4 %shard_map.265 = (f32[2,345600]{1,0:T(2,128)}, f32[2,27648]{1,0:T(2,128)}) custom-call(s32[4]{0:T(128)S(1)} %broadcast_2_me_ref.2.me_ref, bf16[2,2,96,1152]{3,2,1,0:T(8,128)(2,1)S(1)} %get-tuple-element.221.mine_ref, bf16[2,2,96,1152]{3,2,1,0:T(8,128)(2,1)S(1)} %get-tuple-element.220.twin_ref), custom_call_target="tpu_custom_call" | custom-call | flops 3000000000 | bytes 1048576 | tf_op jit(solution)/shard_map/pallas_call | solution.py:68
  261.8 1.9 shard_map.269
  270.7 2.3 collective-permute-start.61
  273.0 2.8 shard_map.270
  275.8 3.0 collective-permute-done.63
  278.8 11.5 %collective-permute-done.62 = bf16[96,1152]{1,0:T(8,128)(2,1)S(1)} collective-permute-done((bf16[96,1152]{1,0:T(8,128)(2,1)S(1)}, bf16[96,1152]{1,0:T(8,128)(2,1)S(1)}, u32[]{:S(2)}, u32[]{:S(2)}) %collective-permute-start.62) | collective-permute-done | bytes 221216 | tf_op jit(solution)/shard_map/ppermute | solution.py:665
  293.3 2.0 collective-permute-start.66
  295.4 2.3 collective-permute-start.67
  313.5 2.7 collective-permute-done.69
  318.3 2.2 shard_map.271
  320.5 4.4 %shard_map.272 = (f32[2,345600]{1,0:T(2,128)}, f32[2,27648]{1,0:T(2,128)}) custom-call(s32[4]{0:T(128)S(1)} %pad_add_fusion.me_ref.refs_0_, bf16[2,2,96,1152]{3,2,1,0:T(8,128)(2,1)S(1)} %maximum_select_fusion.1.mine_ref, bf16[2,2,96,1152]{3,2,1,0:T(8,128)(2,1)S(1)} %collective-permute-done.75.twin_ref), custom_call_target="tpu_custom_call" | custom-call | flops 3000000000 | bytes 1048576 | tf_op jit(solution)/shard_map/pallas_call | solution.py:68
  (422 shorter events, 135.3 us)
Async XLA Ops:
  7.2 59.4 %all-gather.6.cloned.1.call-start = ((), (), s32[]{:S(2)}) async-start(), calls=%async_computation.5 | async-start | bytes 2785280 | tf_op jit(solution)/shard_map/all_gather | solution.py:816
  14.1 179.6 %reduce-scatter.3.cloned.1.call-start = ((), (), s32[]{:S(2)}) async-start(), calls=%async_computation.2 | async-start | bytes 1105920 | tf_op jit(solution)/shard_map/reduce_scatter | solution.py:693
  15.8 9.1 %collective-permute-start.2 = (bf16[80,528]{1,0:T(8,128)(2,1)}, bf16[80,528]{1,0:T(8,128)(2,1)S(1)}, u32[]{:S(2)}, u32[]{:S(2)}) collective-permute-start(bf16[80,528]{1,0:T(8,128)(2,1)} %constant_dynamic-slice_fusion.8), channel_id=1, source_target_pairs={{0,3},{1,2},{2,1},{3,0},{4,7},{5,6},{6,5},{7,4},{8,11},{9,10},{10,... | collective-permute-start | bytes 253448 | tf_op jit(solution)/shard_map/ppermute | solution.py:651
  20.8 13.9 %collective-permute-start.1 = (bf16[80,528]{1,0:T(8,128)(2,1)}, bf16[80,528]{1,0:T(8,128)(2,1)S(1)}, u32[]{:S(2)}, u32[]{:S(2)}) collective-permute-start(bf16[80,528]{1,0:T(8,128)(2,1)} %constant_dynamic-slice_fusion.8), channel_id=1, source_target_pairs={{0,2},{1,3},{2,0},{3,1},{4,6},{5,7},{6,4},{7,5},{8,10},{9,11},{10,... | collective-permute-start | bytes 253448 | tf_op jit(solution)/shard_map/ppermute | solution.py:651
  20.8 13.9 %collective-permute-start = (bf16[80,528]{1,0:T(8,128)(2,1)}, bf16[80,528]{1,0:T(8,128)(2,1)}, u32[]{:S(2)}, u32[]{:S(2)}) collective-permute-start(bf16[80,528]{1,0:T(8,128)(2,1)} %constant_dynamic-slice_fusion.8), channel_id=1, source_target_pairs={{0,1},{1,0},{2,3},{3,2},{4,5},{5,4},{6,7},{7,6},{8,9},{9,8},{10,11... | collective-permute-start | bytes 253448 | tf_op jit(solution)/shard_map/ppermute | solution.py:651
  24.9 10.4 %collective-permute-start.5 = (bf16[80,528]{1,0:T(8,128)(2,1)S(1)}, bf16[80,528]{1,0:T(8,128)(2,1)S(1)}, u32[]{:S(2)}, u32[]{:S(2)}) collective-permute-start(bf16[80,528]{1,0:T(8,128)(2,1)S(1)} %collective-permute-done.2.p3), channel_id=1, source_target_pairs={{0,4},{4,0},{8,12},{12,8},{16,20},{20,16},{24,28},{28,24},{1,5},{5... | collective-permute-start | bytes 253448 | tf_op jit(solution)/shard_map/ppermute | solution.py:684
  45.9 7.9 %collective-permute-start.10 = (f32[2,448]{1,0:T(2,128)S(1)}, f32[2,448]{1,0:T(2,128)S(1)}, u32[]{:S(2)}, u32[]{:S(2)}) collective-permute-start(f32[2,448]{1,0:T(2,128)S(1)} %add.158.s0), channel_id=1, source_target_pairs={{0,3},{1,2},{2,1},{3,0},{4,7},{5,6},{6,5},{7,4},{8,11},{9,10},{10,... | collective-permute-start | bytes 10760 | tf_op jit(solution)/shard_map/ppermute | solution.py:651
  66.6 6.7 %collective-permute-start.13 = (bf16[4,64,4320]{2,1,0:T(8,128)(2,1)}, bf16[4,64,4320]{2,1,0:T(8,128)(2,1)S(1)}, u32[]{:S(2)}, u32[]{:S(2)}) collective-permute-start(bf16[4,64,4320]{2,1,0:T(8,128)(2,1)} %bitcast.175), channel_id=1, source_target_pairs={{0,4},{4,0},{8,12},{12,8},{16,20},{20,16},{24,28},{28,24},{1,5},{5... | collective-permute-start | bytes 6635528 | tf_op jit(solution)/shard_map/ppermute | solution.py:858
  67.0 13.4 %collective-permute-start.12 = (bf16[512,320]{1,0:T(8,128)(2,1)S(1)}, bf16[512,320]{1,0:T(8,128)(2,1)S(1)}, u32[]{:S(2)}, u32[]{:S(2)}) collective-permute-start(bf16[512,320]{1,0:T(8,128)(2,1)S(1)} %get-tuple-element.227), channel_id=1, source_target_pairs={{1,0},{2,1},{3,2},{5,4},{6,5},{7,6},{9,8},{10,9},{11,10},{13,12},{... | collective-permute-start | bytes 983048 | tf_op jit(solution)/shard_map/ppermute | solution.py:719
  68.5 13.1 %collective-permute-start.11 = (bf16[512,320]{1,0:T(8,128)(2,1)S(1)}, bf16[512,320]{1,0:T(8,128)(2,1)S(1)}, u32[]{:S(2)}, u32[]{:S(2)}) collective-permute-start(bf16[512,320]{1,0:T(8,128)(2,1)S(1)} %get-tuple-element.228), channel_id=1, source_target_pairs={{0,1},{1,2},{2,3},{4,5},{5,6},{6,7},{8,9},{9,10},{10,11},{12,13},{... | collective-permute-start | bytes 983048 | tf_op jit(solution)/shard_map/ppermute | solution.py:719
  96.4 5.4 %collective-permute-start.18 = (f32[2,576]{1,0:T(2,128)S(1)}, f32[2,576]{1,0:T(2,128)S(1)}, u32[]{:S(2)}, u32[]{:S(2)}) collective-permute-start(f32[2,576]{1,0:T(2,128)S(1)} %add.160.refs_4_), channel_id=1, source_target_pairs={{0,3},{1,2},{2,1},{3,0},{4,7},{5,6},{6,5},{7,4},{8,11},{9,10},{10,... | collective-permute-start | bytes 13832 | tf_op jit(solution)/shard_map/ppermute | solution.py:651
  121.5 5.4 %collective-permute-start.23 = (f32[2,448]{1,0:T(2,128)S(1)}, f32[2,448]{1,0:T(2,128)S(1)}, u32[]{:S(2)}, u32[]{:S(2)}) collective-permute-start(f32[2,448]{1,0:T(2,128)S(1)} %add.162.s0), channel_id=1, source_target_pairs={{0,3},{1,2},{2,1},{3,0},{4,7},{5,6},{6,5},{7,4},{8,11},{9,10},{10,... | collective-permute-start | bytes 10760 | tf_op jit(solution)/shard_map/ppermute | solution.py:651
  128.3 7.1 %collective-permute-start.26 = (bf16[128,256]{1,0:T(8,128)(2,1)S(1)}, bf16[128,256]{1,0:T(8,128)(2,1)S(1)}, u32[]{:S(2)}, u32[]{:S(2)}) collective-permute-start(bf16[128,256]{1,0:T(8,128)(2,1)S(1)} %get-tuple-element.246), channel_id=1, source_target_pairs={{0,3},{1,2},{2,1},{3,0},{4,7},{5,6},{6,5},{7,4},{8,11},{9,10},{10,... | collective-permute-start | bytes 196616 | tf_op jit(solution)/shard_map/ppermute | solution.py:665
  130.8 7.6 %collective-permute-start.25 = (bf16[128,256]{1,0:T(8,128)(2,1)S(1)}, bf16[128,256]{1,0:T(8,128)(2,1)S(1)}, u32[]{:S(2)}, u32[]{:S(2)}) collective-permute-start(bf16[128,256]{1,0:T(8,128)(2,1)S(1)} %get-tuple-element.247), channel_id=1, source_target_pairs={{0,2},{1,3},{2,0},{3,1},{4,6},{5,7},{6,4},{7,5},{8,10},{9,11},{10,... | collective-permute-start | bytes 196616 | tf_op jit(solution)/shard_map/ppermute | solution.py:665
  131.9 6.5 %collective-permute-start.24 = (bf16[128,256]{1,0:T(8,128)(2,1)S(1)}, bf16[128,256]{1,0:T(8,128)(2,1)S(1)}, u32[]{:S(2)}, u32[]{:S(2)}) collective-permute-start(bf16[128,256]{1,0:T(8,128)(2,1)S(1)} %get-tuple-element.248), channel_id=1, source_target_pairs={{0,1},{1,0},{2,3},{3,2},{4,5},{5,4},{6,7},{7,6},{8,9},{9,8},{10,11... | collective-permute-start | bytes 196616 | tf_op jit(solution)/shard_map/ppermute | solution.py:665
  132.8 13.6 %collective-permute-start.31 = (bf16[128,256]{1,0:T(8,128)(2,1)S(1)}, bf16[128,256]{1,0:T(8,128)(2,1)S(1)}, u32[]{:S(2)}, u32[]{:S(2)}) collective-permute-start(bf16[128,256]{1,0:T(8,128)(2,1)S(1)} %get-tuple-element.242), channel_id=1, source_target_pairs={{0,3},{1,2},{2,1},{3,0},{4,7},{5,6},{6,5},{7,4},{8,11},{9,10},{10,... | collective-permute-start | bytes 196616 | tf_op jit(solution)/shard_map/ppermute | solution.py:665
  135.2 11.1 %collective-permute-start.30 = (bf16[128,256]{1,0:T(8,128)(2,1)S(1)}, bf16[128,256]{1,0:T(8,128)(2,1)S(1)}, u32[]{:S(2)}, u32[]{:S(2)}) collective-permute-start(bf16[128,256]{1,0:T(8,128)(2,1)S(1)} %get-tuple-element.243), channel_id=1, source_target_pairs={{0,2},{1,3},{2,0},{3,1},{4,6},{5,7},{6,4},{7,5},{8,10},{9,11},{10,... | collective-permute-start | bytes 196616 | tf_op jit(solution)/shard_map/ppermute | solution.py:665
  135.5 10.9 %collective-permute-start.29 = (bf16[128,256]{1,0:T(8,128)(2,1)S(1)}, bf16[128,256]{1,0:T(8,128)(2,1)S(1)}, u32[]{:S(2)}, u32[]{:S(2)}) collective-permute-start(bf16[128,256]{1,0:T(8,128)(2,1)S(1)} %get-tuple-element.244), channel_id=1, source_target_pairs={{0,1},{1,0},{2,3},{3,2},{4,5},{5,4},{6,7},{7,6},{8,9},{9,8},{10,11... | collective-permute-start | bytes 196616 | tf_op jit(solution)/shard_map/ppermute | solution.py:665
  147.8 9.2 %collective-permute-start.36 = (bf16[128,256]{1,0:T(8,128)(2,1)S(1)}, bf16[128,256]{1,0:T(8,128)(2,1)S(1)}, u32[]{:S(2)}, u32[]{:S(2)}) collective-permute-start(bf16[128,256]{1,0:T(8,128)(2,1)S(1)} %get-tuple-element.238), channel_id=1, source_target_pairs={{0,3},{1,2},{2,1},{3,0},{4,7},{5,6},{6,5},{7,4},{8,11},{9,10},{10,... | collective-permute-start | bytes 196616 | tf_op jit(solution)/shard_map/ppermute | solution.py:665
  150.0 7.0 %collective-permute-start.35 = (bf16[128,256]{1,0:T(8,128)(2,1)S(1)}, bf16[128,256]{1,0:T(8,128)(2,1)S(1)}, u32[]{:S(2)}, u32[]{:S(2)}) collective-permute-start(bf16[128,256]{1,0:T(8,128)(2,1)S(1)} %get-tuple-element.239), channel_id=1, source_target_pairs={{0,2},{1,3},{2,0},{3,1},{4,6},{5,7},{6,4},{7,5},{8,10},{9,11},{10,... | collective-permute-start | bytes 196616 | tf_op jit(solution)/shard_map/ppermute | solution.py:665
  150.0 7.0 %collective-permute-start.34 = (bf16[128,256]{1,0:T(8,128)(2,1)S(1)}, bf16[128,256]{1,0:T(8,128)(2,1)S(1)}, u32[]{:S(2)}, u32[]{:S(2)}) collective-permute-start(bf16[128,256]{1,0:T(8,128)(2,1)S(1)} %get-tuple-element.240), channel_id=1, source_target_pairs={{0,1},{1,0},{2,3},{3,2},{4,5},{5,4},{6,7},{7,6},{8,9},{9,8},{10,11... | collective-permute-start | bytes 196616 | tf_op jit(solution)/shard_map/ppermute | solution.py:665
  162.3 93.4 %all-gather.4.cloned.1.call-start = ((), (), s32[]{:S(2)}) async-start(), calls=%async_computation.3 | async-start | bytes 1990656 | tf_op jit(solution)/shard_map/all_gather | solution.py:707
  162.4 6.6 %collective-permute-start.39 = (bf16[128,256]{1,0:T(8,128)(2,1)S(1)}, bf16[128,256]{1,0:T(8,128)(2,1)S(1)}, u32[]{:S(2)}, u32[]{:S(2)}) collective-permute-start(bf16[128,256]{1,0:T(8,128)(2,1)S(1)} %get-tuple-element.234), channel_id=1, source_target_pairs={{0,3},{1,2},{2,1},{3,0},{4,7},{5,6},{6,5},{7,4},{8,11},{9,10},{10,... | collective-permute-start | bytes 196616 | tf_op jit(solution)/shard_map/ppermute | solution.py:665
  164.6 5.9 %collective-permute-start.38 = (bf16[128,256]{1,0:T(8,128)(2,1)S(1)}, bf16[128,256]{1,0:T(8,128)(2,1)S(1)}, u32[]{:S(2)}, u32[]{:S(2)}) collective-permute-start(bf16[128,256]{1,0:T(8,128)(2,1)S(1)} %get-tuple-element.235), channel_id=1, source_target_pairs={{0,2},{1,3},{2,0},{3,1},{4,6},{5,7},{6,4},{7,5},{8,10},{9,11},{10,... | collective-permute-start | bytes 196616 | tf_op jit(solution)/shard_map/ppermute | solution.py:665
  164.6 5.9 %collective-permute-start.37 = (bf16[128,256]{1,0:T(8,128)(2,1)S(1)}, bf16[128,256]{1,0:T(8,128)(2,1)S(1)}, u32[]{:S(2)}, u32[]{:S(2)}) collective-permute-start(bf16[128,256]{1,0:T(8,128)(2,1)S(1)} %get-tuple-element.236), channel_id=1, source_target_pairs={{0,1},{1,0},{2,3},{3,2},{4,5},{5,4},{6,7},{7,6},{8,9},{9,8},{10,11... | collective-permute-start | bytes 196616 | tf_op jit(solution)/shard_map/ppermute | solution.py:665
  176.6 5.6 %collective-permute-start.44 = (f32[2,1536]{1,0:T(2,128)S(1)}, f32[2,1536]{1,0:T(2,128)S(1)}, u32[]{:S(2)}, u32[]{:S(2)}) collective-permute-start(f32[2,1536]{1,0:T(2,128)S(1)} %add.168.refs_4_), channel_id=1, source_target_pairs={{0,3},{1,2},{2,1},{3,0},{4,7},{5,6},{6,5},{7,4},{8,11},{9,10},{10,... | collective-permute-start | bytes 36872 | tf_op jit(solution)/shard_map/ppermute | solution.py:651
  193.6 73.5 %reduce-scatter.5.cloned.1.call-start = ((), (), s32[]{:S(2)}) async-start(), calls=%async_computation.4 | async-start | bytes 4423680 | tf_op jit(solution)/shard_map/reduce_scatter | solution.py:693
  193.7 6.5 %collective-permute-start.51 = (f32[2,576]{1,0:T(2,128)S(1)}, f32[2,576]{1,0:T(2,128)S(1)}, u32[]{:S(2)}, u32[]{:S(2)}) collective-permute-start(f32[2,576]{1,0:T(2,128)S(1)} %add.170.refs_5_), channel_id=1, source_target_pairs={{0,3},{1,2},{2,1},{3,0},{4,7},{5,6},{6,5},{7,4},{8,11},{9,10},{10,... | collective-permute-start | bytes 13832 | tf_op jit(solution)/shard_map/ppermute | solution.py:651
  221.6 19.2 %collective-permute-start.53 = (bf16[512,320]{1,0:T(8,128)(2,1)}, bf16[512,320]{1,0:T(8,128)(2,1)S(1)}, u32[]{:S(2)}, u32[]{:S(2)}) collective-permute-start(bf16[512,320]{1,0:T(8,128)(2,1)} %pad_maximum_fusion), channel_id=1, source_target_pairs={{1,0},{2,1},{3,2},{5,4},{6,5},{7,6},{9,8},{10,9},{11,10},{13,12},{... | collective-permute-start | bytes 983048 | tf_op jit(solution)/shard_map/ppermute | solution.py:719
  223.0 17.8 %collective-permute-start.52 = (bf16[512,320]{1,0:T(8,128)(2,1)}, bf16[512,320]{1,0:T(8,128)(2,1)S(1)}, u32[]{:S(2)}, u32[]{:S(2)}) collective-permute-start(bf16[512,320]{1,0:T(8,128)(2,1)} %pad_maximum_fusion.1), channel_id=1, source_target_pairs={{0,1},{1,2},{2,3},{4,5},{5,6},{6,7},{8,9},{9,10},{10,11},{12,13},{... | collective-permute-start | bytes 983048 | tf_op jit(solution)/shard_map/ppermute | solution.py:719
  228.4 19.3 %collective-permute-start.48 = (bf16[1,4,40,832]{3,2,1,0:T(8,128)(2,1)}, bf16[1,4,40,832]{3,2,1,0:T(8,128)(2,1)}, u32[]{:S(2)}, u32[]{:S(2)}) collective-permute-start(bf16[1,4,40,832]{3,2,1,0:T(8,128)(2,1)} %constant_dynamic-slice_fusion.3), channel_id=1, source_target_pairs={{0,8},{4,12},{8,0},{12,4},{16,24},{20,28},{24,16},{28,20},{1,9},{5... | collective-permute-start | bytes 798728 | tf_op jit(solution)/shard_map/ppermute | solution.py:730
  251.3 10.4 %collective-permute-start.58 = (f32[2,448]{1,0:T(2,128)S(1)}, f32[2,448]{1,0:T(2,128)S(1)}, u32[]{:S(2)}, u32[]{:S(2)}) collective-permute-start(f32[2,448]{1,0:T(2,128)S(1)} %add.174.refs_4_), channel_id=1, source_target_pairs={{0,3},{1,2},{2,1},{3,0},{4,7},{5,6},{6,5},{7,4},{8,11},{9,10},{10,... | collective-permute-start | bytes 10760 | tf_op jit(solution)/shard_map/ppermute | solution.py:651
  251.6 10.1 %collective-permute-start.57 = (f32[2,448]{1,0:T(2,128)S(1)}, f32[2,448]{1,0:T(2,128)S(1)}, u32[]{:S(2)}, u32[]{:S(2)}) collective-permute-start(f32[2,448]{1,0:T(2,128)S(1)} %add.174.refs_4_), channel_id=1, source_target_pairs={{0,2},{1,3},{2,0},{3,1},{4,6},{5,7},{6,4},{7,5},{8,10},{9,11},{10,... | collective-permute-start | bytes 10760 | tf_op jit(solution)/shard_map/ppermute | solution.py:651
  254.4 7.4 %collective-permute-start.56 = (f32[2,448]{1,0:T(2,128)S(1)}, f32[2,448]{1,0:T(2,128)S(1)}, u32[]{:S(2)}, u32[]{:S(2)}) collective-permute-start(f32[2,448]{1,0:T(2,128)S(1)} %add.174.refs_4_), channel_id=1, source_target_pairs={{0,1},{1,0},{2,3},{3,2},{4,5},{5,4},{6,7},{7,6},{8,9},{9,8},{10,11... | collective-permute-start | bytes 10760 | tf_op jit(solution)/shard_map/ppermute | solution.py:651
  264.3 11.5 %collective-permute-start.64 = (f32[2,2,1024]{2,1,0:T(2,128)S(1)}, f32[2,2,1024]{2,1,0:T(2,128)S(1)}, u32[]{:S(2)}, u32[]{:S(2)}) collective-permute-start(f32[2,2,1024]{2,1,0:T(2,128)S(1)} %get-tuple-element.255), channel_id=1, source_target_pairs={{0,16},{4,20},{8,24},{12,28},{16,0},{20,4},{24,8},{28,12},{1,17},{... | collective-permute-start | bytes 49160 | tf_op jit(solution)/shard_map/ppermute | solution.py:646
  268.3 7.5 %collective-permute-start.60 = (bf16[1,4,40,528]{3,2,1,0:T(8,128)(2,1)S(1)}, bf16[1,4,40,528]{3,2,1,0:T(8,128)(2,1)S(1)}, u32[]{:S(2)}, u32[]{:S(2)}) collective-permute-start(bf16[1,4,40,528]{3,2,1,0:T(8,128)(2,1)S(1)} %constant_dynamic-slice_fusion.1), channel_id=1, source_target_pairs={{0,8},{4,12},{8,0},{12,4},{16,24},{20,28},{24,16},{28,20},{1,9},{5... | collective-permute-start | bytes 506888 | tf_op jit(solution)/shard_map/ppermute | solution.py:730
  268.6 10.2 %collective-permute-start.63 = (bf16[96,1152]{1,0:T(8,128)(2,1)S(1)}, bf16[96,1152]{1,0:T(8,128)(2,1)S(1)}, u32[]{:S(2)}, u32[]{:S(2)}) collective-permute-start(bf16[96,1152]{1,0:T(8,128)(2,1)S(1)} %get-tuple-element.224), channel_id=1, source_target_pairs={{0,3},{1,2},{2,1},{3,0},{4,7},{5,6},{6,5},{7,4},{8,11},{9,10},{10,... | collective-permute-start | bytes 663560 | tf_op jit(solution)/shard_map/ppermute | solution.py:665
  268.8 21.4 %collective-permute-start.62 = (bf16[96,1152]{1,0:T(8,128)(2,1)S(1)}, bf16[96,1152]{1,0:T(8,128)(2,1)S(1)}, u32[]{:S(2)}, u32[]{:S(2)}) collective-permute-start(bf16[96,1152]{1,0:T(8,128)(2,1)S(1)} %get-tuple-element.225), channel_id=1, source_target_pairs={{0,2},{1,3},{2,0},{3,1},{4,6},{5,7},{6,4},{7,5},{8,10},{9,11},{10,... | collective-permute-start | bytes 663560 | tf_op jit(solution)/shard_map/ppermute | solution.py:665
  270.7 20.3 %collective-permute-start.61 = (bf16[96,1152]{1,0:T(8,128)(2,1)S(1)}, bf16[96,1152]{1,0:T(8,128)(2,1)}, u32[]{:S(2)}, u32[]{:S(2)}) collective-permute-start(bf16[96,1152]{1,0:T(8,128)(2,1)S(1)} %get-tuple-element.226), channel_id=1, source_target_pairs={{0,1},{1,0},{2,3},{3,2},{4,5},{5,4},{6,7},{7,6},{8,9},{9,8},{10,11... | collective-permute-start | bytes 663560 | tf_op jit(solution)/shard_map/ppermute | solution.py:665
  293.2 9.7 %collective-permute-start.65 = (bf16[40,1408]{1,0:T(8,128)(2,1)S(1)}, bf16[40,1408]{1,0:T(8,128)(2,1)S(1)}, u32[]{:S(2)}, u32[]{:S(2)}) collective-permute-start(bf16[40,1408]{1,0:T(8,128)(2,1)S(1)} %get-tuple-element.229), channel_id=1, source_target_pairs={{0,1},{1,0},{2,3},{3,2},{4,5},{5,4},{6,7},{7,6},{8,9},{9,8},{10,11... | collective-permute-start | bytes 337928 | tf_op jit(solution)/shard_map/ppermute | solution.py:665
  293.3 11.3 %collective-permute-start.66 = (bf16[40,1408]{1,0:T(8,128)(2,1)S(1)}, bf16[40,1408]{1,0:T(8,128)(2,1)S(1)}, u32[]{:S(2)}, u32[]{:S(2)}) collective-permute-start(bf16[40,1408]{1,0:T(8,128)(2,1)S(1)} %get-tuple-element.230), channel_id=1, source_target_pairs={{0,2},{1,3},{2,0},{3,1},{4,6},{5,7},{6,4},{7,5},{8,10},{9,11},{10,... | collective-permute-start | bytes 337928 | tf_op jit(solution)/shard_map/ppermute | solution.py:665
  295.4 9.3 %collective-permute-start.67 = (bf16[40,1408]{1,0:T(8,128)(2,1)S(1)}, bf16[40,1408]{1,0:T(8,128)(2,1)S(1)}, u32[]{:S(2)}, u32[]{:S(2)}) collective-permute-start(bf16[40,1408]{1,0:T(8,128)(2,1)S(1)} %get-tuple-element.231), channel_id=1, source_target_pairs={{0,3},{1,2},{2,1},{3,0},{4,7},{5,6},{6,5},{7,4},{8,11},{9,10},{10,... | collective-permute-start | bytes 337928 | tf_op jit(solution)/shard_map/ppermute | solution.py:665
  300.0 7.0 %collective-permute-start.72 = (bf16[96,1152]{1,0:T(8,128)(2,1)S(1)}, bf16[96,1152]{1,0:T(8,128)(2,1)S(1)}, u32[]{:S(2)}, u32[]{:S(2)}) collective-permute-start(bf16[96,1152]{1,0:T(8,128)(2,1)S(1)} %add_convert_fusion.3), channel_id=1, source_target_pairs={{0,16},{4,20},{8,24},{12,28},{16,0},{20,4},{24,8},{28,12},{1,17},{... | collective-permute-start | bytes 663560 | tf_op jit(solution)/shard_map/ppermute | solution.py:646
  301.2 7.3 %collective-permute-start.71 = (bf16[96,1152]{1,0:T(8,128)(2,1)S(1)}, bf16[96,1152]{1,0:T(8,128)(2,1)S(1)}, u32[]{:S(2)}, u32[]{:S(2)}) collective-permute-start(bf16[96,1152]{1,0:T(8,128)(2,1)S(1)} %add_convert_fusion.3), channel_id=1, source_target_pairs={{0,8},{4,12},{8,0},{12,4},{16,24},{20,28},{24,16},{28,20},{1,9},{5... | collective-permute-start | bytes 663560 | tf_op jit(solution)/shard_map/ppermute | solution.py:1018
  304.8 5.3 %collective-permute-start.68 = (bf16[1,40,1408]{2,1,0:T(8,128)(2,1)S(1)}, bf16[1,40,1408]{2,1,0:T(8,128)(2,1)S(1)}, u32[]{:S(2)}, u32[]{:S(2)}) collective-permute-start(bf16[1,40,1408]{2,1,0:T(8,128)(2,1)S(1)} %bitcast.209), channel_id=1, source_target_pairs={{0,16},{4,20},{8,24},{12,28},{16,0},{20,4},{24,8},{28,12},{1,17},{... | collective-permute-start | bytes 337928 | tf_op jit(solution)/shard_map/ppermute | solution.py:646
  307.0 5.1 %collective-permute-start.73 = (bf16[48,1152]{1,0:T(8,128)(2,1)S(1)}, bf16[48,1152]{1,0:T(8,128)(2,1)S(1)}, u32[]{:S(2)}, u32[]{:S(2)}) collective-permute-start(bf16[48,1152]{1,0:T(8,128)(2,1)S(1)} %slice.254), channel_id=1, source_target_pairs={{0,8},{4,12},{8,0},{12,4},{16,24},{20,28},{24,16},{28,20},{1,9},{5... | collective-permute-start | bytes 331784 | tf_op jit(solution)/shard_map/ppermute | solution.py:1028
  308.6 4.8 %collective-permute-start.74 = (bf16[48,1152]{1,0:T(8,128)(2,1)S(1)}, bf16[48,1152]{1,0:T(8,128)(2,1)S(1)}, u32[]{:S(2)}, u32[]{:S(2)}) collective-permute-start(bf16[48,1152]{1,0:T(8,128)(2,1)S(1)} %slice.255), channel_id=1, source_target_pairs={{0,16},{4,20},{8,24},{12,28},{16,0},{20,4},{24,8},{28,12},{1,17},{... | collective-permute-start | bytes 331784 | tf_op jit(solution)/shard_map/ppermute | solution.py:646
  310.1 6.0 %collective-permute-start.69 = (bf16[2,1,40,1408]{3,2,1,0:T(8,128)(2,1)S(1)}, bf16[2,1,40,1408]{3,2,1,0:T(8,128)(2,1)S(1)}, u32[]{:S(2)}, u32[]{:S(2)}) collective-permute-start(bf16[2,1,40,1408]{3,2,1,0:T(8,128)(2,1)S(1)} %maximum_select_fusion.5), channel_id=1, source_target_pairs={{0,8},{4,12},{8,0},{12,4},{16,24},{20,28},{24,16},{28,20},{1,9},{5... | collective-permute-start | bytes 675848 | tf_op jit(solution)/shard_map/ppermute | solution.py:756
  (98 other events, 454.1 us)
Sparse Core Ops, SparseCore 0:
  14.2 52.3 all-gather.5
  162.5 23.5 reduce-scatter.2
  193.8 26.2 all-gather.3
  222.7 40.4 reduce-scatter.4
where the time goes:
time: 336 us; the launch traced here: 332 us
  starting transfers between devices  96.7 us (29%)
  waiting for transfers between devices  82.9 us (25%)
  Pallas kernels  62.7 us (19%)
  local copies, waits for them, and re-layouts  38.3 us (11%)
  matrix products  24.1 us (7%)
  between operations  15.7 us (5%)
  other arithmetic  11.2 us (3%)
    pallas_call x28, Pallas kernels, call(): pl.pallas_call(whole if lazy else body, out_shape=outs, in_specs=specs, o...  62.7 us
    ppermute x21, starting transfers between devices, blk_peers(): lax.ppermute(value, 'blk', xor_pairs('blk', k))  33.3 us
    ppermute x18, starting transfers between devices, swap_blk(): lax.ppermute(mine[k], 'blk', xor_pairs('blk', k))  27.1 us
    conv_general_dilated x6, matrix products, conv(): lax.conv_general_dilated(values, kernel.reshape(-1, 3, 3, *kernel.shape[1...  24.1 us
    ppermute x16, waiting for transfers between devices, dp_sum(): value = value + lax.ppermute(value, 'dp', xor_pairs('dp', step))  23.4 us
    unnamed x141, local copies, waits for them, and re-layouts  21.1 us
    ppermute x18, waiting for transfers between devices, swap_blk(): lax.ppermute(mine[k], 'blk', xor_pairs('blk', k))  19.6 us
    ppermute x21, waiting for transfers between devices, blk_peers(): lax.ppermute(value, 'blk', xor_pairs('blk', k))  18.4 us
  transfers between devices with their start and end apart: 80, of which 43 were waited for; matrix products, arithmetic and copies ran while one was open for 12% of the time, Pallas kernels for 12%

commit v1 on v0

--- a/solution.py
+++ b/solution.py
@@ -190,8 +190,8 @@
 def kernels4_body(me_ref, mine_ref, twin_ref, all_ref, first_ref, last_ref, buf, sems):
     first = pltpu.make_async_copy(all_ref.at[0:9], first_ref, sems.at[0])
     last = pltpu.make_async_copy(all_ref.at[18:27], last_ref, sems.at[1])
-    buf[:, pl.ds(pl.multiple_of(48 * me_ref[2], 16), 48), :] = mine_ref[:, :48, :]
-    buf[:, pl.ds(pl.multiple_of(48 * (1 - me_ref[2]), 16), 48), :] = twin_ref[:, :48, :]
+    buf[:, pl.ds(pl.multiple_of(48 * me_ref[2], 16), 48), :] = mine_ref[...]
+    buf[:, pl.ds(pl.multiple_of(48 * (1 - me_ref[2]), 16), 48), :] = twin_ref[...]
     for t in range(TAPS):
         all_ref[t] = tap_block([buf.at[z] for z in range(4)], t)
         if t == 8:
@@ -219,12 +219,8 @@
     return (parts[0][...] + parts[1][...]) + (parts[2][...] + parts[3][...])
 
 
-def front5_body(me_ref, mine_ref, twin_ref, w_ref, n_ref, own_ref, buf):
-    for src, odd in ((mine_ref, me_ref[2]), (twin_ref, 1 - me_ref[2])):
-        for j in range(5):
-            rows = pl.ds(pl.multiple_of(80 * odd + 16 * j, 16), 16)
-            buf[:, rows, :] = src[:, 48:64, LAYER * j : LAYER * (j + 1)]
-    front_parts(buf, w_ref, n_ref)
+def front5_body(me_ref, shards_ref, w_ref, n_ref, own_ref):
+    front_parts(shards_ref, w_ref, n_ref)
     norms = n_ref[...]
     own = jnp.zeros((2, 256), F32)
     gap = jnp.zeros((2, 16 + POOL_LANE), F32)
@@ -266,7 +262,10 @@
             rim_ref[f, rows, BP:] = silu(y).astype(BF)
 
 
-def pool4_body(pp_ref, before_ref, after_ref, pool_ref, m_ref):
+def pool4_body(pp_ref, before_ref, after_ref, pool_ref, m_ref, pad_ref):
+    pad_ref[0] = before_ref[:, BP:]
+    pad_ref[1:3] = pp_ref[:, :, BP:]
+    pad_ref[3] = after_ref[:, BP:]
     matrix = pool_matrix(256, 8)
     m_ref[...] = jnp.zeros_like(m_ref)
     for f in range(2):
@@ -510,7 +509,8 @@
         turned[:, 512 * f : 512 * f + 512] = dv_ref[f].astype(F32).T.astype(BF)
     for n in range(9):
         for q in range(4):
-            a = before_ref[...] if q == 0 else after_ref[...] if q == 3 else a_ref[q - 1]
+            rim = before_ref if q == 0 else after_ref
+            a = rim[:, BP:] if q in (0, 3) else a_ref[q - 1]
             patches[n % 2, q] = shifted(wide_lanes(a), 8, n // 3 - 1, n % 3 - 1).astype(BF)
         for i in range(3):
             window = patches[n % 2, i : i + 2].reshape(1024, 256)
@@ -809,11 +809,8 @@
 
     packed = lax.dynamic_slice_in_dim(pack_branch(early), index % 2 * 48, 48, 0)
     pieces = gather_pieces(pack_front(after(early, packed), c_first))
-    late_front = lax.dynamic_slice_in_dim(pack_front(late, LAYER, BP), index % 2 * 80, 80, 0)
-    late_front = late_front.reshape(5, 16, LAYER).transpose(1, 0, 2).reshape(16, 5 * LAYER)
-    late_front = jnp.pad(late_front, ((0, 0), (0, packed.shape[1] - 5 * LAYER)))
-    packed = jnp.concatenate([packed, late_front])
     packed = lax.all_gather(packed, "blk", tiled=False)
+    late_front = pack_front(late, LAYER, BP)
     late = after(late, pieces[0])
     taps_5 = call(kernels5_body, shape_of((TAPS, 128, INNER), BF), pack_branch(late), micros=2)
     x = after(x, taps_5)
@@ -847,7 +844,7 @@
     at5 = functools.partial(functools.partial, voxels=late_voxels)
 
     parts = tower_parts(m)
-    z_then = after(z, cot_mine)
+    z_then = after(z, (cot_mine, late_front))
     a, rims, sf4 = call(
         at4(act4_body),
         (shape_of((2, 512, INNER), BF), shape_of((2, 512, BP + INNER), BF), shape_of((2, REDUCED))),
@@ -855,6 +852,7 @@
     )
     before, behind = rim_swap(rims[0], rims[1])
     packed = after(packed, a)
+    late_front = lax.all_gather(after(late_front, packed), "blk", tiled=False)
     twin = lax.ppermute(packed, "dp", xor_pairs("dp", 1))
     taps_4, taps_first, taps_last = call(
         kernels4_body,
@@ -866,16 +864,17 @@
         scratch=[pltpu.VMEM((4, 96, 4320), BF), pltpu.SemaphoreType.DMA((2,))],
     )
     before, behind = after((before, behind), taps_4)
-    pool, m_pool = call(
-        pool4_body, (shape_of((2, 512, BP)), shape_of((2, BP))), rims, before, behind, micros=2
-    )
-    before, behind = before[:, BP:], behind[:, BP:]
-    a_pad = jnp.concatenate([before[None], a, behind[None]]).reshape(4, n, height, breadth, INNER)
+    pool, m_pool, a_pad = call(
+        pool4_body,
+        (shape_of((2, 512, BP)), shape_of((2, BP)), shape_of((4, 512, INNER), BF)),
+        rims, before, behind, micros=1,
+    )
+    a_pad = a_pad.reshape(4, n, height, breadth, INNER)
     c = conv(a_pad, taps_4, flat_pads, forth).reshape(2, 512, OUTER)
     front_5, n5f, n5 = call(
         front5_body,
         (shape_of((576, LAYER), BF), shape_of((2, 1024)), shape_of((2, 256))),
-        me, packed, twin, micros=1, scratch=[pltpu.VMEM((4, 160, LAYER), BF)],
+        me, late_front, micros=1,
     )
     cots = swap_blk([after(cot_mine, c)[k] for k in range(4)])
     parts = tower_parts(call(moments_body, shape_of((2, 576)), c, m_pool, micros=1))
@@ -953,7 +952,7 @@
             shape_of((2, 512, OUTER), BF), shape_of((2, 512, BP), BF),
             shape_of((2, 512, OUTER), BF), shape_of((2, 576)),
         ),
-        gm, c, pool, sb4, nb4, *parts, micros=3, lazy=(0, 1, 2, 3, 4),
+        gm, c, pool, sb4, nb4, *parts, micros=0, lazy=(1, 2, 3, 4),
     )
     image = (1, n, height, breadth, OUTER)
     rim_first = conv(turned4[1].reshape(image), taps_first, flat_pads, back).reshape(512, INNER)
@@ -965,7 +964,7 @@
         kernel_grad4_body,
         shape_of((4, 4, 96, 1152), BF),
         me, a, before, behind, after(dv, (rim_first, rim_last)),
-        micros=8, mib=10,
+        micros=0, mib=10,
         scratch=[pltpu.VMEM((2, 4, 512, 256), BF), pltpu.VMEM((OUTER, 1024), BF)],
     )
     turned4 = after(turned4, (branch_part4, both5))

time: 336 us -> 328 us (0.976)
  waiting for transfers between devices: 82.9 us -> 74.2 us
  local copies, waits for them, and re-layouts: 38.3 us -> 43.8 us
    all_gather x1, waiting for transfers between devices: 10.7 us -> 2.49 us  [on_device(): packed = lax.all_gather(packed, 'blk', tiled=False)]
    ppermute x21, waiting for transfers between devices: 18.4 us -> 11.7 us  [blk_peers(): lax.ppermute(value, 'blk', xor_pairs('blk', k))]
    unnamed x141 -> x133, local copies, waits for them, and re-layouts: 21.1 us -> 26.1 us
  transfers between devices with their start and end apart: 80 -> 81, of which waited for: 43 -> 43; matrix products, arithmetic and copies ran while one was open for 12% -> 14% of each run, Pallas kernels for 12% -> 12%
where the time goes in v1:
time: 328 us; the launch traced here: 325 us
  starting transfers between devices  94.8 us (29%)
  waiting for transfers between devices  74.2 us (23%)
  Pallas kernels  62.7 us (19%)
  local copies, waits for them, and re-layouts  43.8 us (13%)
  matrix products  24.2 us (7%)
  between operations  15.7 us (5%)
  other arithmetic  9.34 us (3%)
    pallas_call x28, Pallas kernels, call(): pl.pallas_call(whole if lazy else body, out_shape=outs, in_specs=specs, o...  62.7 us
    ppermute x21, starting transfers between devices, blk_peers(): lax.ppermute(value, 'blk', xor_pairs('blk', k))  34.7 us
    ppermute x18, starting transfers between devices, swap_blk(): lax.ppermute(mine[k], 'blk', xor_pairs('blk', k))  26.4 us
    unnamed x133, local copies, waits for them, and re-layouts  26.1 us
    ppermute x16, waiting for transfers between devices, dp_sum(): value = value + lax.ppermute(value, 'dp', xor_pairs('dp', step))  25.1 us
    conv_general_dilated x6, matrix products, conv(): lax.conv_general_dilated(values, kernel.reshape(-1, 3, 3, *kernel.shape[1...  24.2 us
    ppermute x18, waiting for transfers between devices, swap_blk(): lax.ppermute(mine[k], 'blk', xor_pairs('blk', k))  17.9 us
    ppermute x4, starting transfers between devices, rim_swap(): return (lax.ppermute(last, 'blk', ahead), lax.ppermute(first, 'blk', back))  11.8 us
  transfers between devices with their start and end apart: 81, of which 43 were waited for; matrix products, arithmetic and copies ran while one was open for 14% of the time, Pallas kernels for 12%

profile of v1, /device:TPU:0, one launch (start us, length us, event | category | flops | bytes accessed | tf_op | source)
XLA Modules:
  0.0 324.7 jit_solution(11631012765149148338)
XLA Ops:
  8.4 2.2 reshape.390
  14.1 5.1 %collective-permute-start.2 = (bf16[80,528]{1,0:T(8,128)(2,1)S(1)}, bf16[80,528]{1,0:T(8,128)(2,1)S(1)}, u32[]{:S(2)}, u32[]{:S(2)}) collective-permute-start(bf16[80,528]{1,0:T(8,128)(2,1)S(1)} %constant_dynamic-slice_fusion.8), channel_id=1, source_target_pairs={{0,3},{1,2},{2,1},{3,0},{4,7},{5,6},{6,5},{7,4},{8,11},{9,10},{10,... | collective-permute-start | bytes 253448 | tf_op jit(solution)/shard_map/ppermute | solution.py:651
  20.5 2.2 reshape.384
  25.9 4.1 %collective-permute-done.1.p2 = bf16[80,528]{1,0:T(8,128)(2,1)S(1)} collective-permute-done((bf16[80,528]{1,0:T(8,128)(2,1)S(1)}, bf16[80,528]{1,0:T(8,128)(2,1)S(1)}, u32[]{:S(2)}, u32[]{:S(2)}) %collective-permute-start.1) | collective-permute-done | bytes 84512 | tf_op jit(solution)/shard_map/ppermute | solution.py:651
  32.8 2.0 shard_map.246
  40.5 6.3 %collective-permute-start.10 = (f32[2,448]{1,0:T(2,128)S(1)}, f32[2,448]{1,0:T(2,128)S(1)}, u32[]{:S(2)}, u32[]{:S(2)}) collective-permute-start(f32[2,448]{1,0:T(2,128)S(1)} %add.154.s0), channel_id=1, source_target_pairs={{0,3},{1,2},{2,1},{3,0},{4,7},{5,6},{6,5},{7,4},{8,11},{9,10},{10,... | collective-permute-start | bytes 10760 | tf_op jit(solution)/shard_map/ppermute | solution.py:651
  53.0 2.5 all-gather.8.cloned.1.call-done
  57.8 4.6 %collective-permute-start.11 = (bf16[512,320]{1,0:T(8,128)(2,1)}, bf16[512,320]{1,0:T(8,128)(2,1)S(1)}, u32[]{:S(2)}, u32[]{:S(2)}) collective-permute-start(bf16[512,320]{1,0:T(8,128)(2,1)} %get-tuple-element.232), channel_id=1, source_target_pairs={{0,1},{1,2},{2,3},{4,5},{5,6},{6,7},{8,9},{9,10},{10,11},{12,13},{... | collective-permute-start | bytes 983048 | tf_op jit(solution)/shard_map/ppermute | solution.py:719
  62.7 3.9 %shard_map.249 = (bf16[27,448,192]{2,1,0:T(8,128)(2,1)S(1)}, bf16[9,448,192]{2,1,0:T(8,128)(2,1)S(1)}, bf16[9,448,192]{2,1,0:T(8,128)(2,1)S(1)}) custom-call(s32[4]{0:T(128)S(1)} %pad_add_fusion.me_ref.refs_0_, bf16[4,48,4320]{2,1,0:T(8,128)(2,1)S(1)} %bitcast.182, bf16[4,48,4320]{2,1,0:T(8,128)(2,1)} %collective-permute-done.13.twin_ref), custom_call_target="tpu_custom_call" | custom-call | flops 5000000000 | bytes 1048576 | tf_op jit(solution)/shard_map/pallas_call | solution.py:68
  70.1 4.2 %collective-permute-done.11.before_ref = bf16[512,320]{1,0:T(8,128)(2,1)S(1)} collective-permute-done((bf16[512,320]{1,0:T(8,128)(2,1)}, bf16[512,320]{1,0:T(8,128)(2,1)S(1)}, u32[]{:S(2)}, u32[]{:S(2)}) %collective-permute-start.11) | collective-permute-done | bytes 327712 | tf_op jit(solution)/shard_map/ppermute | solution.py:719
  76.3 7.5 %fusion.3 = f32[2,8,8,8,448]{4,1,3,2,0:T(8,128)S(1)} fusion(bf16[3,3,3,448,192]{4,3,2,1,0:T(8,128)(2,1)S(1)} %bitcast.173, bf16[4,8,8,8,192]{4,3,2,1,0:T(8,128)(2,1)S(1)} %bitcast.186), kind=kOutput, calls=%fused_computation.11 | convolution fusion | flops 3996647424 | bytes 7266304 | tf_op jit(solution)/shard_map/conv_general_dilated | solution.py:831
  87.9 2.3 collective-permute-done.15
  97.9 12.6 %shard_map.253 = (bf16[128,832]{1,0:T(8,128)(2,1)S(1)}, f32[128,576]{1,0:T(8,128)S(1)}, f32[2,448]{1,0:T(2,128)S(1)}, f32[2,576]{1,0:T(2,128)S(1)}) custom-call(f32[2,512,576]{2,1,0:T(8,128)S(1)} %copy-done.5, f32[2,512,448]{2,1,0:T(8,128)S(1)} %bitcast.168, f32[2,512,128]{2,1,0:T(8,128)S(1)} %get-tuple-element.117.refs_2_.refs_11_, ...), custom_call_target="tpu_custom_call" | custom-call | flops 4000000000 | bytes 1048576 | tf_op jit(solution)/shard_map/pallas_call | solution.py:68
  113.1 2.3 collective-permute-done.20
  122.8 2.1 collective-permute-start.26
  127.3 2.1 collective-permute-start.31
  133.9 2.1 fusion.21
  138.8 2.2 collective-permute-done.28
  142.4 2.1 collective-permute-start.36
  144.5 2.3 collective-permute-start.34
  149.4 2.2 collective-permute-done.33
  154.6 2.3 shard_map.260
  157.0 2.2 collective-permute-start.39
  159.1 2.3 collective-permute-start.37
  169.8 2.3 collective-permute-done.41
  172.1 2.1 collective-permute-start.44
  174.3 2.3 collective-permute-start.42
  178.8 2.6 shard_map.263
  184.7 2.2 collective-permute-done.46
  193.0 2.1 add_convert_fusion
  197.2 2.6 shard_map.266
  205.8 7.9 %shard_map.267 = bf16[4,4,96,1152]{3,2,1,0:T(8,128)(2,1)S(1)} custom-call(s32[4]{0:T(128)S(1)} %pad_add_fusion.me_ref.refs_0_, bf16[2,512,192]{2,1,0:T(8,128)(2,1)S(1)} %copy-done.11, bf16[512,320]{1,0:T(8,128)(2,1)S(1)} %copy-done.20, bf16[512,320]{1,0:T(8,128)(2,1)S(1)} %copy-done.18, bf16[2,512,448]{2,1,0:T(8,128)(2,1)S(1)} %get-tuple-element.160.dv_ref), custom_call_target="tpu_custom_call" | custom-call | tf_op jit(solution)/shard_map/pallas_call | solution.py:68
  217.1 4.6 %collective-permute-start.52 = (bf16[512,320]{1,0:T(8,128)(2,1)S(1)}, bf16[512,320]{1,0:T(8,128)(2,1)S(1)}, u32[]{:S(2)}, u32[]{:S(2)}) collective-permute-start(bf16[512,320]{1,0:T(8,128)(2,1)S(1)} %pad_maximum_fusion.1), channel_id=1, source_target_pairs={{0,1},{1,2},{2,3},{4,5},{5,6},{6,7},{8,9},{9,10},{10,11},{12,13},{... | collective-permute-start | bytes 983048 | tf_op jit(solution)/shard_map/ppermute | solution.py:719
  223.5 10.5 %fusion.1 = f32[2,8,8,8,192]{4,1,3,2,0:T(8,128)S(1)} fusion(bf16[3,3,3,448,192]{4,3,2,1,0:T(8,128)(2,1)} %bitcast.174, bf16[2,8,8,8,448]{4,3,2,1,0:T(8,128)(2,1)S(1)} %bitcast.165), kind=kOutput, calls=%fused_computation.9 | convolution fusion | flops 2664431616 | bytes 6348800 | tf_op jit(solution)/shard_map/conv_general_dilated | solution.py:831
  235.0 2.6 shard_map.268
  242.0 2.7 collective-permute-done.55
  244.9 2.7 collective-permute-start.57
  250.7 4.4 %shard_map.265 = (f32[2,345600]{1,0:T(2,128)}, f32[2,27648]{1,0:T(2,128)}) custom-call(s32[4]{0:T(128)S(1)} %broadcast_2_me_ref.2.me_ref, bf16[2,2,96,1152]{3,2,1,0:T(8,128)(2,1)S(1)} %get-tuple-element.225.mine_ref, bf16[2,2,96,1152]{3,2,1,0:T(8,128)(2,1)S(1)} %get-tuple-element.224.twin_ref), custom_call_target="tpu_custom_call" | custom-call | flops 3000000000 | bytes 1048576 | tf_op jit(solution)/shard_map/pallas_call | solution.py:68
  263.8 2.3 collective-permute-start.61
  266.8 2.8 shard_map.270
  269.6 3.0 collective-permute-done.60
  272.6 10.9 %collective-permute-done.62 = bf16[96,1152]{1,0:T(8,128)(2,1)S(1)} collective-permute-done((bf16[96,1152]{1,0:T(8,128)(2,1)S(1)}, bf16[96,1152]{1,0:T(8,128)(2,1)S(1)}, u32[]{:S(2)}, u32[]{:S(2)}) %collective-permute-start.62) | collective-permute-done | bytes 221216 | tf_op jit(solution)/shard_map/ppermute | solution.py:665
  286.6 2.4 collective-permute-start.66
  294.9 3.2 collective-permute-done.66
  304.3 2.1 collective-permute-done.73
  306.5 2.6 collective-permute-done.69
  311.3 2.2 shard_map.271
  313.5 4.4 %shard_map.272 = (f32[2,345600]{1,0:T(2,128)}, f32[2,27648]{1,0:T(2,128)}) custom-call(s32[4]{0:T(128)S(1)} %pad_add_fusion.me_ref.refs_0_, bf16[2,2,96,1152]{3,2,1,0:T(8,128)(2,1)S(1)} %maximum_select_fusion.1.mine_ref, bf16[2,2,96,1152]{3,2,1,0:T(8,128)(2,1)S(1)} %collective-permute-done.75.twin_ref), custom_call_target="tpu_custom_call" | custom-call | flops 3000000000 | bytes 1048576 | tf_op jit(solution)/shard_map/pallas_call | solution.py:68
  (409 shorter events, 137.6 us)
Async XLA Ops:
  7.2 48.3 %all-gather.8.cloned.1.call-start = ((), (), s32[]{:S(2)}) async-start(), calls=%async_computation.5 | async-start | bytes 2088960 | tf_op jit(solution)/shard_map/all_gather | solution.py:812
  13.0 81.6 %all-gather.10.cloned.1.call-start = ((), (), s32[]{:S(2)}) async-start(), calls=%async_computation.6 | async-start | bytes 1433600 | tf_op jit(solution)/shard_map/all_gather | solution.py:855
  14.1 11.7 %collective-permute-start.2 = (bf16[80,528]{1,0:T(8,128)(2,1)S(1)}, bf16[80,528]{1,0:T(8,128)(2,1)S(1)}, u32[]{:S(2)}, u32[]{:S(2)}) collective-permute-start(bf16[80,528]{1,0:T(8,128)(2,1)S(1)} %constant_dynamic-slice_fusion.8), channel_id=1, source_target_pairs={{0,3},{1,2},{2,1},{3,0},{4,7},{5,6},{6,5},{7,4},{8,11},{9,10},{10,... | collective-permute-start | bytes 253448 | tf_op jit(solution)/shard_map/ppermute | solution.py:651
  19.2 10.8 %collective-permute-start.1 = (bf16[80,528]{1,0:T(8,128)(2,1)S(1)}, bf16[80,528]{1,0:T(8,128)(2,1)S(1)}, u32[]{:S(2)}, u32[]{:S(2)}) collective-permute-start(bf16[80,528]{1,0:T(8,128)(2,1)S(1)} %constant_dynamic-slice_fusion.8), channel_id=1, source_target_pairs={{0,2},{1,3},{2,0},{3,1},{4,6},{5,7},{6,4},{7,5},{8,10},{9,11},{10,... | collective-permute-start | bytes 253448 | tf_op jit(solution)/shard_map/ppermute | solution.py:651
  19.2 10.8 %collective-permute-start = (bf16[80,528]{1,0:T(8,128)(2,1)S(1)}, bf16[80,528]{1,0:T(8,128)(2,1)S(1)}, u32[]{:S(2)}, u32[]{:S(2)}) collective-permute-start(bf16[80,528]{1,0:T(8,128)(2,1)S(1)} %constant_dynamic-slice_fusion.8), channel_id=1, source_target_pairs={{0,1},{1,0},{2,3},{3,2},{4,5},{5,4},{6,7},{7,6},{8,9},{9,8},{10,11... | collective-permute-start | bytes 253448 | tf_op jit(solution)/shard_map/ppermute | solution.py:651
  40.5 9.3 %collective-permute-start.10 = (f32[2,448]{1,0:T(2,128)S(1)}, f32[2,448]{1,0:T(2,128)S(1)}, u32[]{:S(2)}, u32[]{:S(2)}) collective-permute-start(f32[2,448]{1,0:T(2,128)S(1)} %add.154.s0), channel_id=1, source_target_pairs={{0,3},{1,2},{2,1},{3,0},{4,7},{5,6},{6,5},{7,4},{8,11},{9,10},{10,... | collective-permute-start | bytes 10760 | tf_op jit(solution)/shard_map/ppermute | solution.py:651
  46.9 4.9 %collective-permute-start.9 = (f32[2,448]{1,0:T(2,128)S(1)}, f32[2,448]{1,0:T(2,128)S(1)}, u32[]{:S(2)}, u32[]{:S(2)}) collective-permute-start(f32[2,448]{1,0:T(2,128)S(1)} %add.154.s0), channel_id=1, source_target_pairs={{0,2},{1,3},{2,0},{3,1},{4,6},{5,7},{6,4},{7,5},{8,10},{9,11},{10,... | collective-permute-start | bytes 10760 | tf_op jit(solution)/shard_map/ppermute | solution.py:651
  55.5 7.2 %collective-permute-start.13 = (bf16[4,48,4320]{2,1,0:T(8,128)(2,1)}, bf16[4,48,4320]{2,1,0:T(8,128)(2,1)}, u32[]{:S(2)}, u32[]{:S(2)}) collective-permute-start(bf16[4,48,4320]{2,1,0:T(8,128)(2,1)} %bitcast.181), channel_id=1, source_target_pairs={{0,4},{4,0},{8,12},{12,8},{16,20},{20,16},{24,28},{28,24},{1,5},{5... | collective-permute-start | bytes 4976648 | tf_op jit(solution)/shard_map/ppermute | solution.py:856
  56.5 13.6 %collective-permute-start.12 = (bf16[512,320]{1,0:T(8,128)(2,1)}, bf16[512,320]{1,0:T(8,128)(2,1)S(1)}, u32[]{:S(2)}, u32[]{:S(2)}) collective-permute-start(bf16[512,320]{1,0:T(8,128)(2,1)} %get-tuple-element.231), channel_id=1, source_target_pairs={{1,0},{2,1},{3,2},{5,4},{6,5},{7,6},{9,8},{10,9},{11,10},{13,12},{... | collective-permute-start | bytes 983048 | tf_op jit(solution)/shard_map/ppermute | solution.py:719
  57.8 16.5 %collective-permute-start.11 = (bf16[512,320]{1,0:T(8,128)(2,1)}, bf16[512,320]{1,0:T(8,128)(2,1)S(1)}, u32[]{:S(2)}, u32[]{:S(2)}) collective-permute-start(bf16[512,320]{1,0:T(8,128)(2,1)} %get-tuple-element.232), channel_id=1, source_target_pairs={{0,1},{1,2},{2,3},{4,5},{5,6},{6,7},{8,9},{9,10},{10,11},{12,13},{... | collective-permute-start | bytes 983048 | tf_op jit(solution)/shard_map/ppermute | solution.py:719
  62.4 124.6 %reduce-scatter.3.cloned.1.call-start = ((), (), s32[]{:S(2)}) async-start(), calls=%async_computation.2 | async-start | bytes 1105920 | tf_op jit(solution)/shard_map/reduce_scatter | solution.py:693
  90.2 6.3 %collective-permute-start.18 = (f32[2,576]{1,0:T(2,128)S(1)}, f32[2,576]{1,0:T(2,128)S(1)}, u32[]{:S(2)}, u32[]{:S(2)}) collective-permute-start(f32[2,576]{1,0:T(2,128)S(1)} %add.156.refs_4_), channel_id=1, source_target_pairs={{0,3},{1,2},{2,1},{3,0},{4,7},{5,6},{6,5},{7,4},{8,11},{9,10},{10,... | collective-permute-start | bytes 13832 | tf_op jit(solution)/shard_map/ppermute | solution.py:651
  115.5 5.4 %collective-permute-start.23 = (f32[2,448]{1,0:T(2,128)S(1)}, f32[2,448]{1,0:T(2,128)S(1)}, u32[]{:S(2)}, u32[]{:S(2)}) collective-permute-start(f32[2,448]{1,0:T(2,128)S(1)} %add.158.s0), channel_id=1, source_target_pairs={{0,3},{1,2},{2,1},{3,0},{4,7},{5,6},{6,5},{7,4},{8,11},{9,10},{10,... | collective-permute-start | bytes 10760 | tf_op jit(solution)/shard_map/ppermute | solution.py:651
  122.8 6.9 %collective-permute-start.26 = (bf16[128,256]{1,0:T(8,128)(2,1)S(1)}, bf16[128,256]{1,0:T(8,128)(2,1)S(1)}, u32[]{:S(2)}, u32[]{:S(2)}) collective-permute-start(bf16[128,256]{1,0:T(8,128)(2,1)S(1)} %get-tuple-element.250), channel_id=1, source_target_pairs={{0,3},{1,2},{2,1},{3,0},{4,7},{5,6},{6,5},{7,4},{8,11},{9,10},{10,... | collective-permute-start | bytes 196616 | tf_op jit(solution)/shard_map/ppermute | solution.py:665
  125.0 7.5 %collective-permute-start.25 = (bf16[128,256]{1,0:T(8,128)(2,1)S(1)}, bf16[128,256]{1,0:T(8,128)(2,1)S(1)}, u32[]{:S(2)}, u32[]{:S(2)}) collective-permute-start(bf16[128,256]{1,0:T(8,128)(2,1)S(1)} %get-tuple-element.251), channel_id=1, source_target_pairs={{0,2},{1,3},{2,0},{3,1},{4,6},{5,7},{6,4},{7,5},{8,10},{9,11},{10,... | collective-permute-start | bytes 196616 | tf_op jit(solution)/shard_map/ppermute | solution.py:665
  125.8 6.7 %collective-permute-start.24 = (bf16[128,256]{1,0:T(8,128)(2,1)S(1)}, bf16[128,256]{1,0:T(8,128)(2,1)S(1)}, u32[]{:S(2)}, u32[]{:S(2)}) collective-permute-start(bf16[128,256]{1,0:T(8,128)(2,1)S(1)} %get-tuple-element.252), channel_id=1, source_target_pairs={{0,1},{1,0},{2,3},{3,2},{4,5},{5,4},{6,7},{7,6},{8,9},{9,8},{10,11... | collective-permute-start | bytes 196616 | tf_op jit(solution)/shard_map/ppermute | solution.py:665
  127.3 13.7 %collective-permute-start.31 = (bf16[128,256]{1,0:T(8,128)(2,1)S(1)}, bf16[128,256]{1,0:T(8,128)(2,1)S(1)}, u32[]{:S(2)}, u32[]{:S(2)}) collective-permute-start(bf16[128,256]{1,0:T(8,128)(2,1)S(1)} %get-tuple-element.246), channel_id=1, source_target_pairs={{0,3},{1,2},{2,1},{3,0},{4,7},{5,6},{6,5},{7,4},{8,11},{9,10},{10,... | collective-permute-start | bytes 196616 | tf_op jit(solution)/shard_map/ppermute | solution.py:665
  129.4 11.6 %collective-permute-start.30 = (bf16[128,256]{1,0:T(8,128)(2,1)S(1)}, bf16[128,256]{1,0:T(8,128)(2,1)S(1)}, u32[]{:S(2)}, u32[]{:S(2)}) collective-permute-start(bf16[128,256]{1,0:T(8,128)(2,1)S(1)} %get-tuple-element.247), channel_id=1, source_target_pairs={{0,2},{1,3},{2,0},{3,1},{4,6},{5,7},{6,4},{7,5},{8,10},{9,11},{10,... | collective-permute-start | bytes 196616 | tf_op jit(solution)/shard_map/ppermute | solution.py:665
  129.7 11.3 %collective-permute-start.29 = (bf16[128,256]{1,0:T(8,128)(2,1)S(1)}, bf16[128,256]{1,0:T(8,128)(2,1)S(1)}, u32[]{:S(2)}, u32[]{:S(2)}) collective-permute-start(bf16[128,256]{1,0:T(8,128)(2,1)S(1)} %get-tuple-element.248), channel_id=1, source_target_pairs={{0,1},{1,0},{2,3},{3,2},{4,5},{5,4},{6,7},{7,6},{8,9},{9,8},{10,11... | collective-permute-start | bytes 196616 | tf_op jit(solution)/shard_map/ppermute | solution.py:665
  142.4 9.2 %collective-permute-start.36 = (bf16[128,256]{1,0:T(8,128)(2,1)S(1)}, bf16[128,256]{1,0:T(8,128)(2,1)S(1)}, u32[]{:S(2)}, u32[]{:S(2)}) collective-permute-start(bf16[128,256]{1,0:T(8,128)(2,1)S(1)} %get-tuple-element.242), channel_id=1, source_target_pairs={{0,3},{1,2},{2,1},{3,0},{4,7},{5,6},{6,5},{7,4},{8,11},{9,10},{10,... | collective-permute-start | bytes 196616 | tf_op jit(solution)/shard_map/ppermute | solution.py:665
  144.5 7.1 %collective-permute-start.35 = (bf16[128,256]{1,0:T(8,128)(2,1)S(1)}, bf16[128,256]{1,0:T(8,128)(2,1)S(1)}, u32[]{:S(2)}, u32[]{:S(2)}) collective-permute-start(bf16[128,256]{1,0:T(8,128)(2,1)S(1)} %get-tuple-element.243), channel_id=1, source_target_pairs={{0,2},{1,3},{2,0},{3,1},{4,6},{5,7},{6,4},{7,5},{8,10},{9,11},{10,... | collective-permute-start | bytes 196616 | tf_op jit(solution)/shard_map/ppermute | solution.py:665
  144.5 7.1 %collective-permute-start.34 = (bf16[128,256]{1,0:T(8,128)(2,1)S(1)}, bf16[128,256]{1,0:T(8,128)(2,1)S(1)}, u32[]{:S(2)}, u32[]{:S(2)}) collective-permute-start(bf16[128,256]{1,0:T(8,128)(2,1)S(1)} %get-tuple-element.244), channel_id=1, source_target_pairs={{0,1},{1,0},{2,3},{3,2},{4,5},{5,4},{6,7},{7,6},{8,9},{9,8},{10,11... | collective-permute-start | bytes 196616 | tf_op jit(solution)/shard_map/ppermute | solution.py:665
  156.9 92.2 %all-gather.6.cloned.1.call-start = ((), (), s32[]{:S(2)}) async-start(), calls=%async_computation.3 | async-start | bytes 1990656 | tf_op jit(solution)/shard_map/all_gather | solution.py:707
  157.0 6.7 %collective-permute-start.39 = (bf16[128,256]{1,0:T(8,128)(2,1)S(1)}, bf16[128,256]{1,0:T(8,128)(2,1)S(1)}, u32[]{:S(2)}, u32[]{:S(2)}) collective-permute-start(bf16[128,256]{1,0:T(8,128)(2,1)S(1)} %get-tuple-element.238), channel_id=1, source_target_pairs={{0,3},{1,2},{2,1},{3,0},{4,7},{5,6},{6,5},{7,4},{8,11},{9,10},{10,... | collective-permute-start | bytes 196616 | tf_op jit(solution)/shard_map/ppermute | solution.py:665
  159.1 5.9 %collective-permute-start.38 = (bf16[128,256]{1,0:T(8,128)(2,1)S(1)}, bf16[128,256]{1,0:T(8,128)(2,1)S(1)}, u32[]{:S(2)}, u32[]{:S(2)}) collective-permute-start(bf16[128,256]{1,0:T(8,128)(2,1)S(1)} %get-tuple-element.239), channel_id=1, source_target_pairs={{0,2},{1,3},{2,0},{3,1},{4,6},{5,7},{6,4},{7,5},{8,10},{9,11},{10,... | collective-permute-start | bytes 196616 | tf_op jit(solution)/shard_map/ppermute | solution.py:665
  159.1 5.9 %collective-permute-start.37 = (bf16[128,256]{1,0:T(8,128)(2,1)S(1)}, bf16[128,256]{1,0:T(8,128)(2,1)S(1)}, u32[]{:S(2)}, u32[]{:S(2)}) collective-permute-start(bf16[128,256]{1,0:T(8,128)(2,1)S(1)} %get-tuple-element.240), channel_id=1, source_target_pairs={{0,1},{1,0},{2,3},{3,2},{4,5},{5,4},{6,7},{7,6},{8,9},{9,8},{10,11... | collective-permute-start | bytes 196616 | tf_op jit(solution)/shard_map/ppermute | solution.py:665
  172.1 5.6 %collective-permute-start.44 = (f32[2,1536]{1,0:T(2,128)S(1)}, f32[2,1536]{1,0:T(2,128)S(1)}, u32[]{:S(2)}, u32[]{:S(2)}) collective-permute-start(f32[2,1536]{1,0:T(2,128)S(1)} %add.164.refs_4_), channel_id=1, source_target_pairs={{0,3},{1,2},{2,1},{3,0},{4,7},{5,6},{6,5},{7,4},{8,11},{9,10},{10,... | collective-permute-start | bytes 36872 | tf_op jit(solution)/shard_map/ppermute | solution.py:651
  187.0 73.5 %reduce-scatter.5.cloned.1.call-start = ((), (), s32[]{:S(2)}) async-start(), calls=%async_computation.4 | async-start | bytes 4423680 | tf_op jit(solution)/shard_map/reduce_scatter | solution.py:693
  188.6 6.5 %collective-permute-start.51 = (f32[2,576]{1,0:T(2,128)S(1)}, f32[2,576]{1,0:T(2,128)S(1)}, u32[]{:S(2)}, u32[]{:S(2)}) collective-permute-start(f32[2,576]{1,0:T(2,128)S(1)} %add.166.refs_5_), channel_id=1, source_target_pairs={{0,3},{1,2},{2,1},{3,0},{4,7},{5,6},{6,5},{7,4},{8,11},{9,10},{10,... | collective-permute-start | bytes 13832 | tf_op jit(solution)/shard_map/ppermute | solution.py:651
  215.7 18.6 %collective-permute-start.53 = (bf16[512,320]{1,0:T(8,128)(2,1)S(1)}, bf16[512,320]{1,0:T(8,128)(2,1)S(1)}, u32[]{:S(2)}, u32[]{:S(2)}) collective-permute-start(bf16[512,320]{1,0:T(8,128)(2,1)S(1)} %pad_maximum_fusion), channel_id=1, source_target_pairs={{1,0},{2,1},{3,2},{5,4},{6,5},{7,6},{9,8},{10,9},{11,10},{13,12},{... | collective-permute-start | bytes 983048 | tf_op jit(solution)/shard_map/ppermute | solution.py:719
  217.1 17.2 %collective-permute-start.52 = (bf16[512,320]{1,0:T(8,128)(2,1)S(1)}, bf16[512,320]{1,0:T(8,128)(2,1)S(1)}, u32[]{:S(2)}, u32[]{:S(2)}) collective-permute-start(bf16[512,320]{1,0:T(8,128)(2,1)S(1)} %pad_maximum_fusion.1), channel_id=1, source_target_pairs={{0,1},{1,2},{2,3},{4,5},{5,6},{6,7},{8,9},{9,10},{10,11},{12,13},{... | collective-permute-start | bytes 983048 | tf_op jit(solution)/shard_map/ppermute | solution.py:719
  221.7 19.4 %collective-permute-start.48 = (bf16[1,4,40,832]{3,2,1,0:T(8,128)(2,1)S(1)}, bf16[1,4,40,832]{3,2,1,0:T(8,128)(2,1)S(1)}, u32[]{:S(2)}, u32[]{:S(2)}) collective-permute-start(bf16[1,4,40,832]{3,2,1,0:T(8,128)(2,1)S(1)} %constant_dynamic-slice_fusion.3), channel_id=1, source_target_pairs={{0,8},{4,12},{8,0},{12,4},{16,24},{20,28},{24,16},{28,20},{1,9},{5... | collective-permute-start | bytes 798728 | tf_op jit(solution)/shard_map/ppermute | solution.py:730
  244.6 10.4 %collective-permute-start.58 = (f32[2,448]{1,0:T(2,128)S(1)}, f32[2,448]{1,0:T(2,128)S(1)}, u32[]{:S(2)}, u32[]{:S(2)}) collective-permute-start(f32[2,448]{1,0:T(2,128)S(1)} %add.170.refs_4_), channel_id=1, source_target_pairs={{0,3},{1,2},{2,1},{3,0},{4,7},{5,6},{6,5},{7,4},{8,11},{9,10},{10,... | collective-permute-start | bytes 10760 | tf_op jit(solution)/shard_map/ppermute | solution.py:651
  244.9 10.2 %collective-permute-start.57 = (f32[2,448]{1,0:T(2,128)S(1)}, f32[2,448]{1,0:T(2,128)S(1)}, u32[]{:S(2)}, u32[]{:S(2)}) collective-permute-start(f32[2,448]{1,0:T(2,128)S(1)} %add.170.refs_4_), channel_id=1, source_target_pairs={{0,2},{1,3},{2,0},{3,1},{4,6},{5,7},{6,4},{7,5},{8,10},{9,11},{10,... | collective-permute-start | bytes 10760 | tf_op jit(solution)/shard_map/ppermute | solution.py:651
  247.6 7.4 %collective-permute-start.56 = (f32[2,448]{1,0:T(2,128)S(1)}, f32[2,448]{1,0:T(2,128)S(1)}, u32[]{:S(2)}, u32[]{:S(2)}) collective-permute-start(f32[2,448]{1,0:T(2,128)S(1)} %add.170.refs_4_), channel_id=1, source_target_pairs={{0,1},{1,0},{2,3},{3,2},{4,5},{5,4},{6,7},{7,6},{8,9},{9,8},{10,11... | collective-permute-start | bytes 10760 | tf_op jit(solution)/shard_map/ppermute | solution.py:651
  257.7 11.9 %collective-permute-start.64 = (f32[2,2,1024]{2,1,0:T(2,128)S(1)}, f32[2,2,1024]{2,1,0:T(2,128)S(1)}, u32[]{:S(2)}, u32[]{:S(2)}) collective-permute-start(f32[2,2,1024]{2,1,0:T(2,128)S(1)} %get-tuple-element.259), channel_id=1, source_target_pairs={{0,16},{4,20},{8,24},{12,28},{16,0},{20,4},{24,8},{28,12},{1,17},{... | collective-permute-start | bytes 49160 | tf_op jit(solution)/shard_map/ppermute | solution.py:646
  261.7 10.9 %collective-permute-start.63 = (bf16[96,1152]{1,0:T(8,128)(2,1)S(1)}, bf16[96,1152]{1,0:T(8,128)(2,1)S(1)}, u32[]{:S(2)}, u32[]{:S(2)}) collective-permute-start(bf16[96,1152]{1,0:T(8,128)(2,1)S(1)} %get-tuple-element.228), channel_id=1, source_target_pairs={{0,3},{1,2},{2,1},{3,0},{4,7},{5,6},{6,5},{7,4},{8,11},{9,10},{10,... | collective-permute-start | bytes 663560 | tf_op jit(solution)/shard_map/ppermute | solution.py:665
  262.3 21.3 %collective-permute-start.62 = (bf16[96,1152]{1,0:T(8,128)(2,1)S(1)}, bf16[96,1152]{1,0:T(8,128)(2,1)S(1)}, u32[]{:S(2)}, u32[]{:S(2)}) collective-permute-start(bf16[96,1152]{1,0:T(8,128)(2,1)S(1)} %get-tuple-element.229), channel_id=1, source_target_pairs={{0,2},{1,3},{2,0},{3,1},{4,6},{5,7},{6,4},{7,5},{8,10},{9,11},{10,... | collective-permute-start | bytes 663560 | tf_op jit(solution)/shard_map/ppermute | solution.py:665
  263.8 20.4 %collective-permute-start.61 = (bf16[96,1152]{1,0:T(8,128)(2,1)S(1)}, bf16[96,1152]{1,0:T(8,128)(2,1)}, u32[]{:S(2)}, u32[]{:S(2)}) collective-permute-start(bf16[96,1152]{1,0:T(8,128)(2,1)S(1)} %get-tuple-element.230), channel_id=1, source_target_pairs={{0,1},{1,0},{2,3},{3,2},{4,5},{5,4},{6,7},{7,6},{8,9},{9,8},{10,11... | collective-permute-start | bytes 663560 | tf_op jit(solution)/shard_map/ppermute | solution.py:665
  266.2 6.4 %collective-permute-start.60 = (bf16[1,4,40,528]{3,2,1,0:T(8,128)(2,1)S(1)}, bf16[1,4,40,528]{3,2,1,0:T(8,128)(2,1)S(1)}, u32[]{:S(2)}, u32[]{:S(2)}) collective-permute-start(bf16[1,4,40,528]{3,2,1,0:T(8,128)(2,1)S(1)} %constant_dynamic-slice_fusion.1), channel_id=1, source_target_pairs={{0,8},{4,12},{8,0},{12,4},{16,24},{20,28},{24,16},{28,20},{1,9},{5... | collective-permute-start | bytes 506888 | tf_op jit(solution)/shard_map/ppermute | solution.py:730
  286.5 8.4 %collective-permute-start.65 = (bf16[40,1408]{1,0:T(8,128)(2,1)S(1)}, bf16[40,1408]{1,0:T(8,128)(2,1)S(1)}, u32[]{:S(2)}, u32[]{:S(2)}) collective-permute-start(bf16[40,1408]{1,0:T(8,128)(2,1)S(1)} %get-tuple-element.233), channel_id=1, source_target_pairs={{0,1},{1,0},{2,3},{3,2},{4,5},{5,4},{6,7},{7,6},{8,9},{9,8},{10,11... | collective-permute-start | bytes 337928 | tf_op jit(solution)/shard_map/ppermute | solution.py:665
  286.6 11.4 %collective-permute-start.66 = (bf16[40,1408]{1,0:T(8,128)(2,1)S(1)}, bf16[40,1408]{1,0:T(8,128)(2,1)S(1)}, u32[]{:S(2)}, u32[]{:S(2)}) collective-permute-start(bf16[40,1408]{1,0:T(8,128)(2,1)S(1)} %get-tuple-element.234), channel_id=1, source_target_pairs={{0,2},{1,3},{2,0},{3,1},{4,6},{5,7},{6,4},{7,5},{8,10},{9,11},{10,... | collective-permute-start | bytes 337928 | tf_op jit(solution)/shard_map/ppermute | solution.py:665
  289.0 9.0 %collective-permute-start.67 = (bf16[40,1408]{1,0:T(8,128)(2,1)S(1)}, bf16[40,1408]{1,0:T(8,128)(2,1)S(1)}, u32[]{:S(2)}, u32[]{:S(2)}) collective-permute-start(bf16[40,1408]{1,0:T(8,128)(2,1)S(1)} %get-tuple-element.235), channel_id=1, source_target_pairs={{0,3},{1,2},{2,1},{3,0},{4,7},{5,6},{6,5},{7,4},{8,11},{9,10},{10,... | collective-permute-start | bytes 337928 | tf_op jit(solution)/shard_map/ppermute | solution.py:665
  293.3 7.1 %collective-permute-start.72 = (bf16[96,1152]{1,0:T(8,128)(2,1)S(1)}, bf16[96,1152]{1,0:T(8,128)(2,1)S(1)}, u32[]{:S(2)}, u32[]{:S(2)}) collective-permute-start(bf16[96,1152]{1,0:T(8,128)(2,1)S(1)} %add_convert_fusion.3), channel_id=1, source_target_pairs={{0,16},{4,20},{8,24},{12,28},{16,0},{20,4},{24,8},{28,12},{1,17},{... | collective-permute-start | bytes 663560 | tf_op jit(solution)/shard_map/ppermute | solution.py:646
  294.5 6.7 %collective-permute-start.71 = (bf16[96,1152]{1,0:T(8,128)(2,1)S(1)}, bf16[96,1152]{1,0:T(8,128)(2,1)S(1)}, u32[]{:S(2)}, u32[]{:S(2)}) collective-permute-start(bf16[96,1152]{1,0:T(8,128)(2,1)S(1)} %add_convert_fusion.3), channel_id=1, source_target_pairs={{0,8},{4,12},{8,0},{12,4},{16,24},{20,28},{24,16},{28,20},{1,9},{5... | collective-permute-start | bytes 663560 | tf_op jit(solution)/shard_map/ppermute | solution.py:1017
  300.5 5.9 %collective-permute-start.73 = (bf16[48,1152]{1,0:T(8,128)(2,1)S(1)}, bf16[48,1152]{1,0:T(8,128)(2,1)S(1)}, u32[]{:S(2)}, u32[]{:S(2)}) collective-permute-start(bf16[48,1152]{1,0:T(8,128)(2,1)S(1)} %slice.246), channel_id=1, source_target_pairs={{0,8},{4,12},{8,0},{12,4},{16,24},{20,28},{24,16},{28,20},{1,9},{5... | collective-permute-start | bytes 331784 | tf_op jit(solution)/shard_map/ppermute | solution.py:1027
  301.2 5.2 %collective-permute-start.74 = (bf16[48,1152]{1,0:T(8,128)(2,1)S(1)}, bf16[48,1152]{1,0:T(8,128)(2,1)S(1)}, u32[]{:S(2)}, u32[]{:S(2)}) collective-permute-start(bf16[48,1152]{1,0:T(8,128)(2,1)S(1)} %slice.247), channel_id=1, source_target_pairs={{0,16},{4,20},{8,24},{12,28},{16,0},{20,4},{24,8},{28,12},{1,17},{... | collective-permute-start | bytes 331784 | tf_op jit(solution)/shard_map/ppermute | solution.py:646
  303.1 6.0 %collective-permute-start.69 = (bf16[2,1,40,1408]{3,2,1,0:T(8,128)(2,1)S(1)}, bf16[2,1,40,1408]{3,2,1,0:T(8,128)(2,1)S(1)}, u32[]{:S(2)}, u32[]{:S(2)}) collective-permute-start(bf16[2,1,40,1408]{3,2,1,0:T(8,128)(2,1)S(1)} %maximum_select_fusion.5), channel_id=1, source_target_pairs={{0,8},{4,12},{8,0},{12,4},{16,24},{20,28},{24,16},{28,20},{1,9},{5... | collective-permute-start | bytes 675848 | tf_op jit(solution)/shard_map/ppermute | solution.py:756
  (95 other events, 490.1 us)
Sparse Core Ops, SparseCore 0:
  13.1 42.3 all-gather.7
  62.5 27.8 all-gather.9
  157.0 23.5 reduce-scatter.2
  187.1 26.2 all-gather.5
  216.0 40.4 reduce-scatter.4
